TPU v7x, 32 devices: a whole 2x2x4 slice. The times are simulated.
32 devices in a mesh: win: 8 (over z, x), frm: 4 (over y, core).
Axes of the slice: x: 2, y: 2, z: 4, core: 2. Of those that a mesh axis runs over, the one named last changes fastest.
Arguments:
- tokens: bfloat16 [64, 512, 1024], P('win', 'frm'), may hold values from -6 to 6
- condition: bfloat16 [64, 1024], P('win'), may hold values from -6 to 6
- doubled: int32 [64], P('win'), may hold values from 0 to 3
- window_count: int32 [8], P('win'), may hold values from 4 to 8, as said below
- w_ada: bfloat16 [1024, 6144], P('win'), may hold values from -0.1875 to 0.1875
- b_ada: bfloat16 [6144], P('win'), may hold values from -3 to 3
- w_qkv: bfloat16 [1024, 3072], P('win'), may hold values from -0.1875 to 0.1875
- w_out: bfloat16 [1024, 1024], P('win'), may hold values from -1.5 to 1.5
- w_up: bfloat16 [1024, 4096], P('win'), may hold values from -0.1875 to 0.1875
- b_up: bfloat16 [4096], P('win'), may hold values from -3 to 3
- w_down: bfloat16 [4096, 1024], P('win'), may hold values from -0.09375 to 0.09375
- b_down: bfloat16 [1024], P('win'), may hold values from -3 to 3
- table_space: float32 [16, 225], replicated, may hold values from -4 to 4
- table_time: float32 [16, 9], replicated, may hold values from -4 to 4
- cotangent: bfloat16 [64, 512, 1024], P('win', 'frm'), may hold values from -6 to 6
Outputs:
- output: bfloat16 [64, 512, 1024], P('win', 'frm')
- grad_tokens: float32 [64, 512, 1024], P('win', 'frm')
- grad_condition: float32 [64, 1024], P('win')
- grad_w_ada: float32 [1024, 6144], P(None, ('win', 'frm'))
- grad_b_ada: float32 [6144], P(('win', 'frm'))
- grad_w_qkv: float32 [1024, 3072], P(None, ('win', 'frm'))
- grad_w_out: float32 [1024, 1024], P(None, ('win', 'frm'))
- grad_w_up: float32 [1024, 4096], P(None, ('win', 'frm'))
- grad_b_up: float32 [4096], P(('win', 'frm'))
- grad_w_down: float32 [4096, 1024], P(('win', 'frm'))
- grad_b_down: float32 [1024], P(('win', 'frm'))
- grad_table_space: float32 [16, 225], replicated
- grad_table_time: float32 [16, 9], replicated
Inputs may be any that keep to these rules, and one draw needn't show every extreme that they name: `window_count`: each index of win has at most 8 live windows, its first ones; some index has exactly 8.
All inputs are finite; a program needn't handle non-finite values.
Results may differ from a plain program's by a relative error of at most 0.018.
Values may be sent and summed in bfloat16 or wider, within the bound.
No kernel may reach another device: no remote copies, remote signals or barrier semaphores. Data moves between devices by JAX's collectives and lax.ppermute only.
A program may use at most 320 MiB of HBM per device.

v0:
```python
import math

import jax
import jax.numpy as jnp
from jax import lax
from jax.sharding import PartitionSpec as P

SIDE = 8
FRAMES = 5


norm_eps = 1e-06
masked_score = -1e30
exact_mode = lax.Precision.HIGHEST


def normalize(values_in):
    centred = values_in - jnp.mean(values_in, axis=-1, keepdims=True)
    inverse = lax.rsqrt(jnp.mean(centred * centred, axis=-1, keepdims=True) + norm_eps)
    return (centred * inverse, inverse)


def normalize_back(grad_normed, normed, inverse):
    return inverse * (
        grad_normed
        - jnp.mean(grad_normed, axis=-1, keepdims=True)
        - normed * jnp.mean(grad_normed * normed, axis=-1, keepdims=True)
    )


def slot_layout(first_row, row_count, doubled, spatial):
    slot_ids = first_row // spatial + jnp.arange(row_count // spatial, dtype=jnp.int32)
    holder_ids = slot_ids // 2
    second_slot = slot_ids % 2
    later = (holder_ids[None, :] > doubled[:, None]).astype(jnp.int32)
    frame_ids = jnp.minimum(holder_ids[None, :] + later + second_slot[None, :], FRAMES - 1)
    slot_live = (second_slot[None, :] == 0) | (holder_ids[None, :] == doubled[:, None])
    return (frame_ids, slot_live)


def space_onehot(side):
    places = jnp.arange(side * side, dtype=jnp.int32)
    across = places // side
    along = places % side
    offset_index = (across[:, None] - across[None, :] + side - 1) * (2 * side - 1) + (
        along[:, None] - along[None, :] + side - 1
    )
    table_ids = jnp.arange((2 * side - 1) * (2 * side - 1), dtype=jnp.int32)
    return (offset_index.reshape(-1)[:, None] == table_ids[None, :]).astype(jnp.float32)


def window_scores(
    query_block, key_block, query_frames, key_frames, key_live, space_bias, time_table
):
    group_size, query_rows, head_count, head_dim = query_block.shape
    key_rows = key_block.shape[1]
    spatial = space_bias.shape[-1]
    time_count = time_table.shape[1]
    raw_scores = jnp.einsum(
        "gqhe,gkhe->ghqk", query_block, key_block, preferred_element_type=jnp.float32
    ) * head_dim ** (-0.5)
    offset = query_frames[:, :, None] - key_frames[:, None, :] + (time_count - 1) // 2
    time_onehot = (offset[..., None] == jnp.arange(time_count, dtype=jnp.int32)).astype(jnp.float32)
    time_bias = jnp.einsum("gabt,ht->ghab", time_onehot, time_table, precision=exact_mode)
    shaped = raw_scores.reshape(
        group_size, head_count, query_rows // spatial, spatial, key_rows // spatial, spatial
    )
    shaped = shaped + space_bias[None, :, None, :, None, :] + time_bias[:, :, :, None, :, None]
    shaped = jnp.where(key_live[:, None, None, None, :, None], shaped, masked_score)
    return (shaped.reshape(group_size, head_count, query_rows, key_rows), time_onehot)


def to_groups(array_in, group_size):
    return array_in.reshape((array_in.shape[0] // group_size, group_size) + array_in.shape[1:])


def from_groups(array_in):
    return array_in.reshape((array_in.shape[0] * array_in.shape[1],) + array_in.shape[2:])


def on_device(
    tokens,
    condition,
    doubled,
    window_count,
    w_ada,
    b_ada,
    w_qkv,
    w_out,
    w_up,
    b_up,
    w_down,
    b_down,
    table_space,
    table_time,
    cotangent,
):
    windows, row_count, model_width = tokens.shape
    head_count = table_space.shape[0]
    head_dim = model_width // head_count
    spatial = SIDE * SIDE
    holder = lax.axis_index("frm")
    group_size = math.gcd(windows, 4)
    scale = head_dim ** (-0.5)

    def grouped_map(function, members):
        result = lax.map(
            function, jax.tree.map(lambda member: to_groups(member, group_size), members)
        )
        return result

    weight_set = (w_ada, b_ada, w_qkv, w_out, w_up, b_up, w_down, b_down)
    gathered = (
        lax.all_gather(weight_set[0], "win", axis=0, tiled=True),
        lax.all_gather(weight_set[1], "win", axis=0, tiled=True),
        lax.all_gather(weight_set[2], "win", axis=0, tiled=True),
        lax.all_gather(weight_set[3], "win", axis=0, tiled=True),
        lax.all_gather(weight_set[4], "win", axis=0, tiled=True),
        lax.all_gather(weight_set[5], "win", axis=0, tiled=True),
        lax.all_gather(weight_set[6], "win", axis=0, tiled=True),
        lax.all_gather(weight_set[7], "win", axis=0, tiled=True),
    )
    ada_full, ada_bias, qkv_full, out_full, up_full, up_bias, down_full, down_bias = gathered
    query_frames, slot_live = slot_layout(holder * row_count, row_count, doubled, spatial)
    window_live = jnp.arange(windows, dtype=jnp.int32) < window_count[0]
    row_live = jnp.repeat((window_live[:, None] & slot_live).astype(jnp.float32), spatial, axis=1)[
        :, :, None
    ]
    onehot_space = space_onehot(SIDE)
    space_bias = jnp.dot(table_space, onehot_space.T, precision=exact_mode).reshape(
        head_count, spatial, spatial
    )
    cond_full = condition.astype(jnp.float32)
    silu_low = jax.nn.silu(cond_full).astype(jnp.bfloat16)
    modulation = jnp.dot(silu_low, ada_full, preferred_element_type=jnp.float32) + ada_bias.astype(
        jnp.float32
    )
    blocks = jnp.split(modulation, 6, axis=-1)
    shift_one, scale_one, gate_one = (
        blocks[0][:, None, :],
        blocks[1][:, None, :],
        blocks[2][:, None, :],
    )
    shift_two, scale_two, gate_two = (
        blocks[3][:, None, :],
        blocks[4][:, None, :],
        blocks[5][:, None, :],
    )
    token_full = tokens.astype(jnp.float32)
    normed_one, inverse_one = normalize(token_full)
    hidden_one = (normed_one * (1.0 + scale_one) + shift_one).astype(jnp.bfloat16)
    hidden_flat = hidden_one.reshape(windows * row_count, model_width)
    projected = jnp.dot(hidden_flat, qkv_full, preferred_element_type=jnp.float32).astype(
        jnp.bfloat16
    )
    projected = projected.reshape(windows, row_count, 3, head_count, head_dim)
    query_heads = projected[:, :, 0]
    key_heads = projected[:, :, 1]
    value_heads = projected[:, :, 2]
    pair_send = projected[:, :, 1:].reshape(windows, row_count, 2 * model_width)
    start_state = (
        jnp.full((windows, head_count, row_count), masked_score, jnp.float32),
        jnp.zeros((windows, head_count, row_count), jnp.float32),
        jnp.zeros((windows, head_count, row_count, head_dim), jnp.float32),
    )
    shard_piece = lax.all_gather(pair_send, "frm", axis=1, tiled=True)
    key_rows = shard_piece.shape[1]
    key_frames, key_live = slot_layout(jnp.int32(0), key_rows, doubled, spatial)
    pair = shard_piece.reshape(windows, key_rows, 2, head_count, head_dim)

    def attend_one_group(grouped):
        (
            top_score,
            denominator,
            summed,
            query_block,
            pair_block,
            query_frame_block,
            key_frame_block,
            key_live_block,
        ) = grouped
        scores, unused_onehot = window_scores(
            query_block,
            pair_block[:, :, 0],
            query_frame_block,
            key_frame_block,
            key_live_block,
            space_bias,
            table_time,
        )
        new_top = jnp.maximum(top_score, jnp.max(scores, axis=-1))
        shrink = jnp.exp(top_score - new_top)
        weights = jnp.exp(scores - new_top[..., None])
        denominator = denominator * shrink + jnp.sum(weights, axis=-1)
        summed = summed * shrink[..., None] + jnp.einsum(
            "ghqk,gkhe->ghqe",
            weights.astype(jnp.bfloat16),
            pair_block[:, :, 1],
            preferred_element_type=jnp.float32,
        )
        return (new_top, denominator, summed)

    members = (
        start_state[0],
        start_state[1],
        start_state[2],
        query_heads,
        pair,
        query_frames,
        key_frames,
        key_live,
    )
    result = grouped_map(attend_one_group, members)
    top_score = from_groups(result[0])
    denominator = from_groups(result[1])
    summed = from_groups(result[2])
    log_total = top_score + jnp.log(denominator)
    attended_full = summed / denominator[..., None]
    attended = (
        jnp.transpose(attended_full, (0, 2, 1, 3))
        .reshape(windows * row_count, model_width)
        .astype(jnp.bfloat16)
    )
    branch_attn = jnp.dot(attended, out_full, preferred_element_type=jnp.float32).reshape(
        windows, row_count, model_width
    )
    mid = token_full + row_live * gate_one * branch_attn
    normed_two, inverse_two = normalize(mid)
    hidden_two = (
        (normed_two * (1.0 + scale_two) + shift_two)
        .astype(jnp.bfloat16)
        .reshape(windows * row_count, model_width)
    )
    pre_act = jnp.dot(hidden_two, up_full, preferred_element_type=jnp.float32) + up_bias.astype(
        jnp.float32
    )
    activated = jax.nn.gelu(pre_act).astype(jnp.bfloat16)
    branch_mlp = (
        jnp.dot(activated, down_full, preferred_element_type=jnp.float32)
        + down_bias.astype(jnp.float32)
    ).reshape(windows, row_count, model_width)
    result = (mid + row_live * gate_two * branch_mlp).astype(jnp.bfloat16)
    ada_back, qkv_back, out_back, up_back, down_back = (
        ada_full,
        qkv_full,
        out_full,
        up_full,
        down_full,
    )
    grad_out = cotangent.astype(jnp.float32)
    grad_mlp = (row_live * gate_two * grad_out).astype(jnp.bfloat16)
    grad_gate_two = jnp.sum(row_live * branch_mlp * grad_out, axis=1)
    grad_mlp_flat = grad_mlp.reshape(windows * row_count, model_width)
    grad_down_w = jnp.dot(activated.T, grad_mlp_flat, preferred_element_type=jnp.float32)
    grad_down_b = jnp.sum(grad_mlp_flat.astype(jnp.float32), axis=0)
    grad_activated = jnp.dot(grad_mlp_flat, down_back.T, preferred_element_type=jnp.float32)
    unused_value, gelu_back = jax.vjp(jax.nn.gelu, pre_act)
    grad_pre = gelu_back(grad_activated)[0].astype(jnp.bfloat16)
    grad_up_w = jnp.dot(hidden_two.T, grad_pre, preferred_element_type=jnp.float32)
    grad_up_b = jnp.sum(grad_pre.astype(jnp.float32), axis=0)
    grad_hidden_two = jnp.dot(grad_pre, up_back.T, preferred_element_type=jnp.float32).reshape(
        windows, row_count, model_width
    )
    grad_shift_two = jnp.sum(grad_hidden_two, axis=1)
    grad_scale_two = jnp.sum(grad_hidden_two * normed_two, axis=1)
    grad_mid = grad_out + normalize_back(
        grad_hidden_two * (1.0 + scale_two), normed_two, inverse_two
    )
    grad_branch = (row_live * gate_one * grad_mid).astype(jnp.bfloat16)
    grad_gate_one = jnp.sum(row_live * branch_attn * grad_mid, axis=1)
    grad_branch_flat = grad_branch.reshape(windows * row_count, model_width)
    grad_out_w = jnp.dot(attended.T, grad_branch_flat, preferred_element_type=jnp.float32)
    grad_attended = jnp.dot(
        grad_branch_flat, out_back.T, preferred_element_type=jnp.float32
    ).astype(jnp.bfloat16)
    grad_heads = grad_attended.reshape(windows, row_count, head_count, head_dim)
    row_dot = jnp.sum(
        grad_heads.astype(jnp.float32) * jnp.transpose(attended_full, (0, 2, 1, 3)), axis=-1
    )
    log_rows = jnp.transpose(log_total, (0, 2, 1))
    stats_log, stats_dot = (
        lax.all_gather(log_rows, "frm", axis=1, tiled=True),
        lax.all_gather(row_dot, "frm", axis=1, tiled=True),
    )
    dot_heads = jnp.transpose(row_dot, (0, 2, 1))
    shard_piece = lax.all_gather(pair_send, "frm", axis=1, tiled=True)
    key_rows = shard_piece.shape[1]
    key_frames, key_live = slot_layout(jnp.int32(0), key_rows, doubled, spatial)
    pair = shard_piece.reshape(windows, key_rows, 2, head_count, head_dim)

    def query_one_group(grouped):
        (
            grad_query,
            query_block,
            grad_block,
            log_block,
            dot_block,
            pair_block,
            query_frame_block,
            key_frame_block,
            key_live_block,
        ) = grouped
        scores, unused_onehot = window_scores(
            query_block,
            pair_block[:, :, 0],
            query_frame_block,
            key_frame_block,
            key_live_block,
            space_bias,
            table_time,
        )
        probs = jnp.exp(scores - log_block[..., None])
        grad_probs = jnp.einsum(
            "gqhe,gkhe->ghqk", grad_block, pair_block[:, :, 1], preferred_element_type=jnp.float32
        )
        grad_scores = (probs * (grad_probs - dot_block[..., None])).astype(jnp.bfloat16)
        return grad_query + jnp.einsum(
            "ghqk,gkhe->ghqe", grad_scores, pair_block[:, :, 0], preferred_element_type=jnp.float32
        )

    members = (
        jnp.zeros((windows, head_count, row_count, head_dim), jnp.float32),
        query_heads,
        grad_heads,
        log_total,
        dot_heads,
        pair,
        query_frames,
        key_frames,
        key_live,
    )
    grad_query_sum = from_groups(grouped_map(query_one_group, members))
    query_send = projected[:, :, 0].reshape(windows, row_count, model_width)
    key_start = (
        jnp.zeros((windows, row_count, head_count, head_dim), jnp.float32),
        jnp.zeros((windows, row_count, head_count, head_dim), jnp.float32),
        jnp.zeros((head_count, spatial, spatial), jnp.float32),
        jnp.zeros(table_time.shape, jnp.float32),
    )
    query_piece = lax.all_gather(query_send, "frm", axis=1, tiled=True)
    grad_piece = lax.all_gather(
        grad_attended.reshape(windows, row_count, model_width), "frm", axis=1, tiled=True
    )
    query_rows = query_piece.shape[1]
    piece_frames, unused_live = slot_layout(jnp.int32(0), query_rows, doubled, spatial)
    piece_log = jnp.transpose(stats_log, (0, 2, 1))
    piece_dot = jnp.transpose(stats_dot, (0, 2, 1))

    def key_one_group(grouped):
        (
            grad_key,
            grad_value,
            query_block,
            grad_block,
            log_block,
            dot_block,
            frame_block,
            key_block,
            value_block,
            key_frame_block,
            key_live_block,
        ) = grouped
        scores, time_onehot = window_scores(
            query_block,
            key_block,
            frame_block,
            key_frame_block,
            key_live_block,
            space_bias,
            table_time,
        )
        probs = jnp.exp(scores - log_block[..., None])
        grad_value = grad_value + jnp.einsum(
            "ghqk,gqhe->gkhe",
            probs.astype(jnp.bfloat16),
            grad_block,
            preferred_element_type=jnp.float32,
        )
        grad_probs = jnp.einsum(
            "gqhe,gkhe->ghqk", grad_block, value_block, preferred_element_type=jnp.float32
        )
        grad_scores = (probs * (grad_probs - dot_block[..., None])).astype(jnp.bfloat16)
        grad_key = grad_key + jnp.einsum(
            "ghqk,gqhe->gkhe", grad_scores, query_block, preferred_element_type=jnp.float32
        )
        local_groups = grad_scores.shape[0]
        shaped = grad_scores.astype(jnp.float32).reshape(
            local_groups, head_count, query_rows // spatial, spatial, row_count // spatial, spatial
        )
        space_part = jnp.sum(shaped, axis=(0, 2, 4))
        slot_part = jnp.sum(shaped, axis=(3, 5))
        time_part = jnp.einsum("ghab,gabt->ht", slot_part, time_onehot, precision=exact_mode)
        return (grad_key, grad_value, space_part, time_part)

    members = (
        key_start[0],
        key_start[1],
        query_piece.reshape(windows, query_rows, head_count, head_dim),
        grad_piece.reshape(windows, query_rows, head_count, head_dim),
        piece_log,
        piece_dot,
        piece_frames,
        key_heads,
        value_heads,
        query_frames,
        slot_live,
    )
    outcome = grouped_map(key_one_group, members)
    grad_key_sum = from_groups(outcome[0])
    grad_value_sum = from_groups(outcome[1])
    grad_space_sum = jnp.sum(outcome[2], axis=0)
    grad_time_sum = jnp.sum(outcome[3], axis=0)
    grad_queries = jnp.transpose(grad_query_sum, (0, 2, 1, 3)) * scale
    grad_projected = jnp.stack([grad_queries, grad_key_sum * scale, grad_value_sum], axis=2).astype(
        jnp.bfloat16
    )
    grad_projected = grad_projected.reshape(windows * row_count, 3 * model_width)
    grad_qkv_w = jnp.dot(hidden_flat.T, grad_projected, preferred_element_type=jnp.float32)
    grad_hidden_one = jnp.dot(
        grad_projected, qkv_back.T, preferred_element_type=jnp.float32
    ).reshape(windows, row_count, model_width)
    grad_shift_one = jnp.sum(grad_hidden_one, axis=1)
    grad_scale_one = jnp.sum(grad_hidden_one * normed_one, axis=1)
    grad_tokens = grad_mid + normalize_back(
        grad_hidden_one * (1.0 + scale_one), normed_one, inverse_one
    )
    grad_mod_part = jnp.concatenate(
        [
            grad_shift_one,
            grad_scale_one,
            grad_gate_one,
            grad_shift_two,
            grad_scale_two,
            grad_gate_two,
        ],
        axis=-1,
    )
    grad_mod = lax.psum(grad_mod_part, "frm").astype(jnp.bfloat16)
    chosen = jnp.arange(windows, dtype=jnp.int32) % lax.axis_size("frm") == holder
    silu_share = jnp.where(chosen[:, None], silu_low, jnp.zeros_like(silu_low))
    grad_ada_w = jnp.dot(silu_share.T, grad_mod, preferred_element_type=jnp.float32)
    grad_ada_b = jnp.sum(jnp.where(chosen[:, None], grad_mod.astype(jnp.float32), 0.0), axis=0)
    unused_silu, silu_back = jax.vjp(jax.nn.silu, cond_full)
    grad_condition = silu_back(jnp.dot(grad_mod, ada_back.T, preferred_element_type=jnp.float32))[0]
    grad_space_table = jnp.dot(
        grad_space_sum.reshape(head_count, spatial * spatial), onehot_space, precision=exact_mode
    )
    table_space_grad, table_time_grad = lax.psum((grad_space_table, grad_time_sum), ("win", "frm"))
    weight_grads = (
        grad_ada_w,
        grad_ada_b,
        grad_qkv_w,
        grad_out_w,
        grad_up_w,
        grad_up_b,
        grad_down_w,
        grad_down_b,
    )
    summed_grads = (
        lax.psum_scatter(weight_grads[0], ("win", "frm"), scatter_dimension=1, tiled=True),
        lax.psum_scatter(weight_grads[1], ("win", "frm"), scatter_dimension=0, tiled=True),
        lax.psum_scatter(weight_grads[2], ("win", "frm"), scatter_dimension=1, tiled=True),
        lax.psum_scatter(weight_grads[3], ("win", "frm"), scatter_dimension=1, tiled=True),
        lax.psum_scatter(weight_grads[4], ("win", "frm"), scatter_dimension=1, tiled=True),
        lax.psum_scatter(weight_grads[5], ("win", "frm"), scatter_dimension=0, tiled=True),
        lax.psum_scatter(weight_grads[6], ("win", "frm"), scatter_dimension=0, tiled=True),
        lax.psum_scatter(weight_grads[7], ("win", "frm"), scatter_dimension=0, tiled=True),
    )
    return (
        result,
        grad_tokens,
        grad_condition,
        summed_grads[0],
        summed_grads[1],
        summed_grads[2],
        summed_grads[3],
        summed_grads[4],
        summed_grads[5],
        summed_grads[6],
        summed_grads[7],
        table_space_grad,
        table_time_grad,
    )


def solution(mesh):
    return jax.shard_map(
        on_device,
        mesh=mesh,
        in_specs=(
            P("win", "frm", None),
            P("win", None),
            P("win"),
            P("win"),
            P("win", None),
            P("win"),
            P("win", None),
            P("win", None),
            P("win", None),
            P("win"),
            P("win", None),
            P("win"),
            P(),
            P(),
            P("win", "frm", None),
        ),
        out_specs=(
            P("win", "frm", None),
            P("win", "frm", None),
            P("win", None),
            P(None, ("win", "frm")),
            P(("win", "frm")),
            P(None, ("win", "frm")),
            P(None, ("win", "frm")),
            P(None, ("win", "frm")),
            P(("win", "frm")),
            P(("win", "frm"), None),
            P(("win", "frm")),
            P(),
            P(),
        ),
        check_vma=False,
    )
```

profile of v0, /device:TPU:9, one launch (start us, length us, event | category | flops | bytes accessed | tf_op | source)
XLA Modules:
  0.0 2209.5 jit_solution(568638920359149111)
XLA Ops:
  9.4 22.9 %all-gather = bf16[8,1,768]{2,1,0:T(2,128)(2,1)S(1)} all-gather(bf16[1,1,768]{2,1,0:T(2,128)(2,1)S(1)} %reshape.516), channel_id=1, replica_groups=mesh['win'=8,'frm'=4] {'win'}, dimensions={0}, use_global_device_ids=true | all-gather | bytes 13824 | tf_op jit(solution)/shard_map/all_gather | solution.py:115
  35.1 150.7 %all-gather.12.cloned.1.call-done = bf16[1024,6144]{1,0:T(8,128)(2,1)} async-done(((bf16[128,6144]{1,0:T(8,128)(2,1)}), bf16[1024,6144]{1,0:T(8,128)(2,1)}) %all-gather.12.cloned.1.call-update) | async-done | bytes 12582928 | tf_op jit(solution)/shard_map/all_gather | solution.py:114
  196.5 88.7 %all-gather.14.cloned.1.call-done = bf16[1024,3072]{1,0:T(8,128)(2,1)} async-done(((bf16[128,3072]{1,0:T(8,128)(2,1)}), bf16[1024,3072]{1,0:T(8,128)(2,1)}) %all-gather.14.cloned.1.call-update) | async-done | bytes 6291472 | tf_op jit(solution)/shard_map/all_gather | solution.py:116
  319.4 21.8 all-gather.1
  341.8 13.0 all-gather.2
  365.4 59.2 %all-gather.16.cloned.1.call-done = bf16[8,512,2048]{1,2,0:T(8,128)(2,1)} async-done(((bf16[8,128,2048]{1,2,0:T(8,128)(2,1)}), bf16[8,512,2048]{1,2,0:T(8,128)(2,1)}) %all-gather.16.cloned.1.call-update) | async-done | bytes 16777232 | tf_op jit(solution)/shard_map/all_gather | solution.py:166
  424.6 14.1 copy.190
  441.3 183.3 %while.40 = (s32[]{:T(128)}, f32[2,4,16,128]{3,2,1,0:T(8,128)S(1)}, f32[2,4,16,128]{3,2,1,0:T(8,128)S(1)}, f32[2,4,16,128,64]{3,4,2,1,0:T(8,128)}, pred[2,4,8]{2...) while((s32[]{:T(128)}, f32[2,4,16,128]{3,2,1,0:T(8,128)S(1)}, ...), condition=%wide.region_5.6_spmd, body=%wide.region_2.5_spmd.sunk | while | flops 1112167168 | bytes 230845296 | solution.py:107
  441.8 11.2 add.671
  452.9 27.9 %add.672 = f32[4,16,128,512]{3,2,1,0:T(8,128)} reshape(f32[4,16,2,64,8,64]{5,4,3,2,1,0:T(8,128)} %add.671) | data formatting | bytes 33554432 | tf_op jit(solution)/shard_map/while/body/eval_jaxpr/add | solution.py:68
  500.9 14.8 fusion.192
  532.9 11.2 add.671
  544.2 27.7 %add.672 = f32[4,16,128,512]{3,2,1,0:T(8,128)} reshape(f32[4,16,2,64,8,64]{5,4,3,2,1,0:T(8,128)} %add.671) | data formatting | bytes 33554432 | tf_op jit(solution)/shard_map/while/body/eval_jaxpr/add | solution.py:68
  591.9 14.5 fusion.192
  606.4 11.2 bitcast_dynamic-update-slice_fusion.11
  644.6 16.1 fusion.133
  660.7 63.2 %all-gather.22.cloned.1.call-done = bf16[4096,1024]{1,0:T(8,128)(2,1)} async-done(((bf16[512,1024]{1,0:T(8,128)(2,1)}), bf16[4096,1024]{1,0:T(8,128)(2,1)}) %all-gather.22.cloned.1.call-update) | async-done | bytes 8388624 | tf_op jit(solution)/shard_map/all_gather | solution.py:120
  724.0 24.8 %convert_reduce_fusion.1 = (f32[4096]{0:T(1024)}, bf16[1024,4096]{1,0:T(8,128)(2,1)}) fusion(f32[1024,4096]{1,0:T(8,128)} %fusion.133, f32[4096]{0:T(1024)S(1)} %bitcast.401, bf16[1024,1024]{1,0:T(8,128)(2,1)S(1)} %bitcast.386, bf16[4096,1024]{1,0:T(8,128)(2,1)} %all-gather.22.cloned.1.call-done), kind=kOutput, calls=%fused_computation.108 | convolution fusion | flops 8686399488 | bytes 35684352 | tf_op jit(solution)/shard_map/dot_general | solution.py:256
  748.8 13.1 fusion.93
  764.3 16.9 broadcast_add_fusion
  849.5 177.0 %while.41 = (s32[]{:T(128)}, f32[2,4,16,128,64]{3,4,2,1,0:T(8,128)}, pred[2,4,8]{2,1,0:T(4,128)(4,1)S(1)}, bf16[2,4,128,16,64]{2,4,3,1,0:T(8,128)(2,1)S(1)}, bf1...) while((s32[]{:T(128)}, ...), condition=%wide.region_12.13_spmd, body=%wide.region_11.12_spmd.sunk | while | flops 1644278528 | bytes 152268144 | solution.py:107
  861.6 28.2 %add.682 = f32[4,16,128,512]{3,2,1,0:T(8,128)} reshape(f32[4,16,2,64,8,64]{5,4,3,2,1,0:T(8,128)} %add.681) | data formatting | bytes 33554432 | tf_op jit(solution)/shard_map/while/body/eval_jaxpr/add | solution.py:68
  920.5 18.2 bitcast_dynamic-update-slice_fusion.12
  950.3 27.6 %add.682 = f32[4,16,128,512]{3,2,1,0:T(8,128)} reshape(f32[4,16,2,64,8,64]{5,4,3,2,1,0:T(8,128)} %add.681) | data formatting | bytes 33554432 | tf_op jit(solution)/shard_map/while/body/eval_jaxpr/add | solution.py:68
  1008.3 18.2 bitcast_dynamic-update-slice_fusion.12
  1035.4 11.4 copy.199
  1046.8 345.7 %while.42 = (s32[]{:T(128)}, f32[2,4,128,16,64]{2,4,3,1,0:T(8,128)}, bf16[2,4,128,16,64]{2,4,3,1,0:T(8,128)(2,1)}, f32[2,16,64,64]{3,2,1,0:T(8,128)}, f32[2,16,9...) while((s32[]{:T(128)}, ...), condition=%wide.region_17.18_spmd, body=%wide.region_13.17_spmd.sunk | while | flops 2197971200 | bytes 328022912 | solution.py:107
  1047.6 12.4 add.691
  1060.0 31.5 %add.692 = f32[4,16,512,128]{3,2,1,0:T(8,128)} reshape(f32[4,16,8,64,2,64]{5,4,3,2,1,0:T(2,128)} %add.691) | data formatting | bytes 33554432 | tf_op jit(solution)/shard_map/while/body/eval_jaxpr/add | solution.py:68
  1111.7 11.4 subtract_exponential_fusion.3
  1123.1 13.3 convert_reduce_fusion.5
  1136.5 28.7 %reshape.537 = f32[4,16,8,64,2,64]{5,4,3,2,1,0:T(2,128)} reshape(bf16[4,16,512,128]{3,2,1,0:T(8,128)(2,1)} %get-tuple-element.886) | data formatting | bytes 25165824 | tf_op jit(solution)/shard_map/while/body/eval_jaxpr/reshape | solution.py:387
  1165.1 17.7 reduce_sum.263
  1220.3 12.4 add.691
  1232.7 31.4 %add.692 = f32[4,16,512,128]{3,2,1,0:T(8,128)} reshape(f32[4,16,8,64,2,64]{5,4,3,2,1,0:T(2,128)} %add.691) | data formatting | bytes 33554432 | tf_op jit(solution)/shard_map/while/body/eval_jaxpr/add | solution.py:68
  1284.3 11.4 subtract_exponential_fusion.3
  1295.6 13.3 convert_reduce_fusion.5
  1309.0 28.6 %reshape.537 = f32[4,16,8,64,2,64]{5,4,3,2,1,0:T(2,128)} reshape(bf16[4,16,512,128]{3,2,1,0:T(8,128)(2,1)} %get-tuple-element.886) | data formatting | bytes 25165824 | tf_op jit(solution)/shard_map/while/body/eval_jaxpr/reshape | solution.py:387
  1337.6 17.7 reduce_sum.263
  1396.7 12.8 copy.204
  1420.3 14.7 fusion.134
  1436.7 20.3 fusion.126
  1458.8 14.0 fusion.86
  1472.9 16.6 all-reduce.5
  1503.2 42.9 %all-reduce.3 = (f32[6144]{0:T(1024)S(1)}, f32[4096]{0:T(1024)S(1)}, f32[1024]{0:T(1024)S(1)}, f32[16,225]{1,0:T(8,128)}, f32[16,9]{1,0:T(8,128)}) all-reduce(f32[6144]{0:T(1024)S(1)} %select_reduce_fusion, f32[4096]{0:T(1024)S(1)} %copy-done.64, f32[1024]{0:T(1024)S(1)} %copy-done.61, ...), channel_id=3, replica_groups=mesh['win'=8,'frm'=4] {'win','frm'}, use_global_device_ids=true, to_apply=%region_29.30.clone | all-reduce | flops 15008 | bytes 120064
  1573.1 189.5 %reduce-scatter.12.cloned.1.call-done = f32[1024,128]{1,0:T(8,128)} async-done(((f32[1024,4096]{1,0:T(8,128)}), f32[1024,128]{1,0:T(8,128)}) %reduce-scatter.12.cloned.1.call-update) | async-done | bytes 524304 | tf_op jit(solution)/shard_map/reduce_scatter | solution.py:464
  1762.6 187.4 %reduce-scatter.14.cloned.1.call-done = f32[128,1024]{1,0:T(8,128)} async-done(((f32[4096,1024]{1,0:T(8,128)}), f32[128,1024]{1,0:T(8,128)}) %reduce-scatter.14.cloned.1.call-update) | async-done | bytes 524304 | tf_op jit(solution)/shard_map/reduce_scatter | solution.py:466
  1950.1 252.5 %reduce-scatter.6.cloned.1.call-done = f32[1024,192]{0,1:T(8,128)} async-done(((f32[1024,6144]{0,1:T(8,128)}), f32[1024,192]{0,1:T(8,128)}) %reduce-scatter.6.cloned.1.call-update) | async-done | bytes 786448 | tf_op jit(solution)/shard_map/reduce_scatter | solution.py:460
  (412 shorter events, 484.3 us)
Async XLA Ops:
  7.2 348.2 %copy-start = (f32[16,225]{1,0:T(8,128)S(1)}, f32[16,225]{1,0:T(8,128)}, u32[]{:S(2)}) copy-start(f32[16,225]{1,0:T(8,128)} %param.33) | copy-start | bytes 43204
  7.2 27.1 %copy-start.10 = (bf16[8,128,1024]{2,1,0:T(8,128)(2,1)S(1)}, bf16[8,128,1024]{2,1,0:T(8,128)(2,1)}, u32[]{:S(2)}) copy-start(bf16[8,128,1024]{2,1,0:T(8,128)(2,1)} %param.21) | copy-start | bytes 6291460
  7.2 178.5 %copy-start.47 = (bf16[8,1024]{1,0:T(8,128)(2,1)S(1)}, bf16[8,1024]{1,0:T(8,128)(2,1)}, u32[]{:S(2)}) copy-start(bf16[8,1024]{1,0:T(8,128)(2,1)} %param.22) | copy-start | bytes 49156
  7.2 178.5 %all-gather.12.cloned.1.call-start = ((), (), s32[]{:S(2)}) async-start(), calls=%async_computation.5 | async-start | bytes 14155776 | tf_op jit(solution)/shard_map/all_gather | solution.py:114
  8.0 277.2 %all-gather.14.cloned.1.call-start = ((), (), s32[]{:S(2)}) async-start(), calls=%async_computation.6 | async-start | bytes 7077888 | tf_op jit(solution)/shard_map/all_gather | solution.py:116
  8.7 415.9 %all-gather.16.cloned.1.call-start = ((), (), s32[]{:S(2)}) async-start(), calls=%async_computation.7 | async-start | bytes 20971520 | tf_op jit(solution)/shard_map/all_gather | solution.py:166
  34.3 158.4 %copy-start.57 = (f32[8,128]{1,0:T(8,128)}, f32[8,128]{1,0:T(8,128)S(1)}, u32[]{:S(2)}) copy-start(f32[8,128]{1,0:T(8,128)S(1)} %broadcast_multiply_fusion.6) | copy-start | bytes 12292
  35.1 157.7 %copy-start.59 = (f32[8,128]{1,0:T(8,128)}, f32[8,128]{1,0:T(8,128)S(1)}, u32[]{:S(2)}) copy-start(f32[8,128]{1,0:T(8,128)S(1)} %add_rsqrt_fusion.1) | copy-start | bytes 12292
  315.3 26.5 %copy-start.79 = (bf16[128]{0:T(256)(128)(2,1)S(1)}, bf16[128]{0:T(256)(128)(2,1)}, u32[]{:S(2)}) copy-start(bf16[128]{0:T(256)(128)(2,1)} %param.32) | copy-start | bytes 772
  315.4 314.4 %all-gather.18.cloned.1.call-start = ((), (), s32[]{:S(2)}) async-start(), calls=%async_computation.8 | async-start | bytes 2359296 | tf_op jit(solution)/shard_map/all_gather | solution.py:117
  315.9 328.7 %all-gather.20.cloned.1.call-start = ((), (), s32[]{:S(2)}) async-start(), calls=%async_computation.9 | async-start | bytes 9437184 | tf_op jit(solution)/shard_map/all_gather | solution.py:118
  316.5 407.5 %all-gather.22.cloned.1.call-start = ((), (), s32[]{:S(2)}) async-start(), calls=%async_computation.10 | async-start | bytes 9437184 | tf_op jit(solution)/shard_map/all_gather | solution.py:120
  317.1 718.3 %all-gather.26.cloned.1.call-start = ((), (), s32[]{:S(2)}) async-start(), calls=%async_computation.12 | async-start | bytes 10485760 | tf_op jit(solution)/shard_map/all_gather | solution.py:341
  317.2 46.3 %copy-start.70 = (s32[2]{0:T(128)}, s32[2]{0:T(128)S(1)}, u32[]{:S(2)}) copy-start(s32[2]{0:T(128)S(1)} %get-tuple-element.617) | copy-start | bytes 28
  317.3 46.3 %copy-start.73 = (pred[2]{0:T(512)(128)(4,1)}, pred[2]{0:T(512)(128)(4,1)S(1)}, u32[]{:S(2)}) copy-start(pred[2]{0:T(512)(128)(4,1)S(1)} %broadcast_compare_fusion.1) | copy-start | bytes 10
  317.7 45.9 %copy-start.62 = (s32[4096]{0:T(1024)}, s32[4096]{0:T(1024)S(1)}, u32[]{:S(2)}) copy-start(s32[4096]{0:T(1024)S(1)} %add.452) | copy-start | bytes 49156
  606.4 13.6 copy-start.2
  624.6 14.9 copy-start.6
  624.6 14.9 copy-start.8
  624.6 14.9 copy-start.34
  624.6 14.9 copy-start.39
  624.6 14.9 copy-start.45
  624.7 14.9 copy-start.49
  624.7 14.9 copy-start.76
  644.6 79.4 %copy-start.21 = (bf16[8,128,1024]{2,1,0:T(8,128)(2,1)S(1)}, bf16[8,128,1024]{2,1,0:T(8,128)(2,1)}, u32[]{:S(2)}) copy-start(bf16[8,128,1024]{2,1,0:T(8,128)(2,1)} %get-tuple-element.581) | copy-start | bytes 6291460
  644.6 79.4 %copy-start.65 = (f32[8,1,512]{2,1,0:T(1,128)S(1)}, f32[8,1,512]{2,1,0:T(1,128)}, u32[]{:S(2)}) copy-start(f32[8,1,512]{2,1,0:T(1,128)} %convert_element_type.159) | copy-start | bytes 49156
  764.3 17.0 copy-start.17
  764.3 17.0 copy-start.18
  793.6 253.2 %all-gather.24.cloned.1.call-start = ((), (), s32[]{:S(2)}) async-start(), calls=%async_computation.11 | async-start | bytes 10485760 | tf_op jit(solution)/shard_map/all_gather | solution.py:340
  797.3 764.8 %reduce-scatter.10.cloned.1.call-start = ((), (), s32[]{:S(2)}) async-start(), calls=%async_computation.15 | async-start | bytes 4325376 | tf_op jit(solution)/shard_map/reduce_scatter | solution.py:463
  824.8 13.9 copy-start.46
  829.7 19.7 copy-start.32
  829.7 19.7 copy-start.7
  829.7 19.7 copy-start.9
  829.7 19.7 copy-start.40
  829.7 19.7 copy-start.50
  829.7 19.7 copy-start.77
  829.7 19.7 copy-start.82
  1035.3 537.8 %reduce-scatter.8.cloned.1.call-start = ((), (), s32[]{:S(2)}) async-start(), calls=%async_computation.14 | async-start | bytes 12976128 | tf_op jit(solution)/shard_map/reduce_scatter | solution.py:462
  1418.8 343.9 %reduce-scatter.12.cloned.1.call-start = ((), (), s32[]{:S(2)}) async-start(), calls=%async_computation.16 | async-start | bytes 17301504 | tf_op jit(solution)/shard_map/reduce_scatter | solution.py:464
  1435.0 515.1 %reduce-scatter.14.cloned.1.call-start = ((), (), s32[]{:S(2)}) async-start(), calls=%async_computation.17 | async-start | bytes 17301504 | tf_op jit(solution)/shard_map/reduce_scatter | solution.py:466
  1457.1 745.5 %reduce-scatter.6.cloned.1.call-start = ((), (), s32[]{:S(2)}) async-start(), calls=%async_computation.13 | async-start | bytes 25952256 | tf_op jit(solution)/shard_map/reduce_scatter | solution.py:460
  1458.7 14.1 copy-start.55
  1458.7 14.1 copy-start.53
  1458.8 14.1 copy-start.52
  1458.8 14.1 copy-start.54
  1458.8 30.7 %copy-start.48 = (bf16[8,1024]{1,0:T(8,128)(2,1)S(1)}, bf16[8,1024]{1,0:T(8,128)(2,1)}, u32[]{:S(2)}) copy-start(bf16[8,1024]{1,0:T(8,128)(2,1)} %param.22) | copy-start | bytes 49156
  1547.9 654.6 %copy-start.1 = (f32[16,225]{1,0:T(8,128)S(1)}, f32[16,225]{1,0:T(8,128)}, u32[]{:S(2)}) copy-start(f32[16,225]{1,0:T(8,128)} %param.33) | copy-start | bytes 43204
  (55 other events, 281.8 us)
Sparse Core Ops, SparseCore 0:
  10.2 175.4 all-gather.11
  187.9 97.2 all-gather.13
  315.5 109.1 all-gather.15
  426.6 48.1 all-gather.17
  476.8 122.0 all-gather.19
  600.8 123.0 all-gather.21
  793.7 61.9 all-gather.25
  857.3 59.3 all-gather.23
  1035.4 116.4 reduce-scatter.9
  1418.9 154.1 reduce-scatter.7
  1576.1 186.5 reduce-scatter.11
  1765.5 184.5 reduce-scatter.13
  1958.2 244.3 reduce-scatter.5
where the time goes:
time: 2230 us; the launch traced here: 2210 us
  waiting for transfers between devices  1010 us (45%)
  local copies, waits for them, and re-layouts  566 us (25%)
  matrix products  379 us (17%)
  blocking collectives  134 us (6%)
  other arithmetic  106 us (5%)
    add x30, local copies, waits for them, and re-layouts, window_scores(): shaped + space_bias[None, :, None, :, None, :]  325 us
    reduce_scatter x1, waiting for transfers between devices, on_device(): lax.psum_scatter(weight_grads[0], ('win', 'frm'), scatter_dimension=1, ti...  252 us
    reduce_scatter x1, waiting for transfers between devices, on_device(): lax.psum_scatter(weight_grads[4], ('win', 'frm'), scatter_dimension=1, ti...  190 us
    reduce_scatter x1, waiting for transfers between devices, on_device(): lax.psum_scatter(weight_grads[6], ('win', 'frm'), scatter_dimension=0, ti...  187 us
    all_gather x1, waiting for transfers between devices, on_device(): lax.all_gather(weight_set[0], 'win', axis=0, tiled=True)  151 us
    all_gather x1, waiting for transfers between devices, on_device(): lax.all_gather(weight_set[2], 'win', axis=0, tiled=True)  88.7 us
    dot_general x6, matrix products, window_scores(): jnp.einsum('gqhe,gkhe->ghqk', query_block, key_block, preferred_element_t...  72.8 us
    all_gather x1, waiting for transfers between devices, on_device(): lax.all_gather(weight_set[6], 'win', axis=0, tiled=True)  63.2 us
  transfers between devices with their start and end apart: 13, of which 8 were waited for; matrix products, arithmetic and copies ran while one was open for 42% of the time, Pallas kernels for 0%

commit v1 on v0

v1 whole, which is shorter than its diff:
```python
import functools

import jax
import jax.numpy as jnp
from jax import lax
from jax.experimental import pallas as pl
from jax.experimental.pallas import tpu as pltpu
from jax.sharding import PartitionSpec as P

SIDE = 8
FRAMES = 5
SPATIAL = SIDE * SIDE
BOTH = ("win", "frm")
EPS = 1e-06
VMEM_LIMIT = 50 * 1024 * 1024

f32 = jnp.float32
bf16 = jnp.bfloat16
exact_mode = lax.Precision.HIGHEST


def swap_frm(array, bit):
    return lax.ppermute(array, "frm", [(j, j ^ bit) for j in range(4)])


def swap_core(array):
    return swap_frm(array, 1)


def swap_y(array):
    return swap_frm(array, 2)


def swap_win(array, bits):
    count = lax.axis_size("win")
    return lax.ppermute(array, "win", [(j, j ^ bits) for j in range(count)])


def exchange_all(array):
    return lax.all_to_all(array, BOTH, split_axis=0, concat_axis=0, tiled=True)


def pick(array, index, axis):
    return lax.dynamic_index_in_dim(array, index, axis, keepdims=False)


def place_kernel(where, *refs):
    count = (len(refs) - 2) // 4
    sources, out, sems = refs[: 4 * count], refs[4 * count], refs[4 * count + 1]
    z, x, y = where[0], where[1], where[2]
    cut = sources[0].shape[-1]
    copies = []
    for core in range(count):
        near_a, far_a, near_b, far_b = sources[4 * core : 4 * core + 4]
        for l in range(2):
            for j in range(2):
                for k in range(4):
                    index = (z ^ k) * 2 + (x ^ j)
                    half = y ^ l
                    own = where[3] ^ core
                    pieces = (
                        ((far_a if l else near_a).at[j, k], pl.ds(0, cut)),
                        (
                            (far_b if j else near_b).at[l, k],
                            pl.ds(cut, out.shape[-1] - cut),
                        ),
                    )
                    for source, columns in pieces:
                        target = (
                            out.at[index, own, half, :, columns]
                            if count == 2
                            else out.at[index, half, :, columns]
                        )
                        copy = pltpu.make_async_copy(source, target, sems.at[len(copies)])
                        copy.start()
                        copies.append(copy)
    for copy in copies:
        copy.wait()


def place(where, pieces, both_cores):
    near_a, near_b = pieces[0], pieces[2]
    rows = near_a.shape[2]
    columns = near_a.shape[3] + near_b.shape[3]
    shape = (8, 2, 2, rows, columns) if both_cores else (8, 2, rows, columns)
    return pl.pallas_call(
        place_kernel,
        out_shape=jax.ShapeDtypeStruct(shape, near_a.dtype),
        in_specs=[pl.BlockSpec(memory_space=pltpu.SMEM)]
        + [pl.BlockSpec(memory_space=pl.ANY)] * len(pieces),
        out_specs=pl.BlockSpec(memory_space=pl.ANY),
        scratch_shapes=[pltpu.SemaphoreType.DMA((8 * len(pieces),))],
        cost_estimate=pl.CostEstimate(
            flops=0, bytes_accessed=4 * near_a.dtype.itemsize * near_a.size, transcendentals=0
        ),
        name="place",
    )(where, *pieces)


def gather_weight(shard, where, both_cores):
    n_win = lax.axis_size("win")
    rows, columns = shard.shape
    if n_win != 8:
        whole = lax.all_gather(shard, "win", axis=0)
        if both_cores:
            other = swap_core(whole)
            first = where[3] == 0
            whole = jnp.stack(
                [jnp.where(first, whole, other), jnp.where(first, other, whole)], axis=1
            )
        return whole
    y = where[2]
    half = pick(shard.reshape(2, rows // 2, columns), y, 0)
    cut = (columns * 3 // 8) // 128 * 128
    along_z = [half] + [swap_win(half, 2 * k) for k in (1, 2, 3)]
    stack_a = jnp.stack([piece[:, :cut] for piece in along_z])
    stack_b = jnp.stack([piece[:, cut:] for piece in along_z])
    arrived_a = swap_win(stack_a, 1)
    arrived_b = swap_y(stack_b)
    near_a = jnp.stack([stack_a, arrived_a])
    near_b = jnp.stack([stack_b, arrived_b])
    far_a = swap_y(near_a)
    far_b = swap_win(near_b, 1)
    pieces = [near_a, far_a, near_b, far_b]
    if both_cores:
        pieces = pieces + [swap_core(piece) for piece in pieces]
        return place(where, pieces, True).reshape(8, 2, rows, columns)
    return place(where, pieces, False).reshape(8, rows, columns)


def add_low(left, right):
    return (left.astype(f32) + right.astype(f32)).astype(bf16)


def scatter_sum(grad, where):
    n_win = lax.axis_size("win")
    z, x, y = where[0], where[1], where[2]
    if n_win != 8:
        mine = lax.psum_scatter(grad.astype(f32), "win", scatter_dimension=0, tiled=False)
        return pick(mine, y, 0) + swap_y(pick(mine, 1 - y, 0))
    rows, columns = grad.shape[2:]
    cube = grad.reshape(4, 2, 2, rows, columns)
    cut = columns // 2
    side_a, side_b = cube[..., :cut], cube[..., cut:]
    got_a = swap_win(pick(side_a, 1 - x, 1), 1)
    got_b = swap_y(pick(side_b, 1 - y, 2))
    own_a = pick(side_a, x, 1)
    own_b = pick(side_b, y, 2)
    more_a = swap_y(add_low(pick(own_a, 1 - y, 1), pick(got_a, 1 - y, 1)))
    more_b = swap_win(add_low(pick(own_b, 1 - x, 1), pick(got_b, 1 - x, 1)), 1)
    kept_a = pick(own_a, y, 1).astype(f32) + pick(got_a, y, 1).astype(f32) + more_a.astype(f32)
    kept_b = pick(own_b, x, 1).astype(f32) + pick(got_b, x, 1).astype(f32) + more_b.astype(f32)
    kept = jnp.concatenate([kept_a.astype(bf16), kept_b.astype(bf16)], axis=-1)
    total = pick(kept, z, 0).astype(f32)
    for k in (1, 2, 3):
        total = total + swap_win(pick(kept, z ^ k, 0), 2 * k).astype(f32)
    return total


def windows_in(array, doubled, y, c):
    width = array.shape[-1]
    split = array.reshape(2, 2, 2, 2, SPATIAL, width)
    other = swap_core(pick(split, 1 - c, 1))
    own = pick(split, c, 1)
    evens_own, evens_other = own[:, :, 0], other[:, :, 0]
    first = c == 0
    even_0 = jnp.where(first, evens_own, evens_other)
    even_1 = jnp.where(first, evens_other, evens_own)
    twice = pick(doubled.reshape(2, 2, 2), c, 1)
    odd = jnp.where((twice == 2 * y + c)[:, :, None, None], own[:, :, 1], other[:, :, 1])
    packed = jnp.stack([even_0, even_1, odd], axis=2)
    away = swap_y(pick(packed, 1 - y, 0))
    here = pick(packed, y, 0)
    low_y = y == 0
    pair_0 = jnp.where(low_y, here[:, :2], away[:, :2])
    pair_1 = jnp.where(low_y, away[:, :2], here[:, :2])
    mine = pick(twice, y, 0)
    last = jnp.where((mine // 2 == y)[:, None, None], here[:, 2], away[:, 2])
    return jnp.concatenate([pair_0, pair_1, last[:, None]], axis=1)


def windows_out(array, y, c):
    evens, last = array[:, :4], array[:, 4:]
    away = jnp.concatenate([jnp.where(y == 0, evens[:, 2:], evens[:, :2]), last], axis=1)
    here = jnp.concatenate([jnp.where(y == 0, evens[:, :2], evens[:, 2:]), last], axis=1)
    back = swap_y(away)
    first = y == 0
    both = jnp.stack([jnp.where(first, here, back), jnp.where(first, back, here)])
    odd = both[:, :, 2]
    mine = jnp.stack([pick(both[:, :, :2], c, 2), odd], axis=2)
    theirs = jnp.stack([pick(both[:, :, :2], 1 - c, 2), odd], axis=2)
    got = swap_core(theirs)
    low_c = c == 0
    whole = jnp.stack([jnp.where(low_c, mine, got), jnp.where(low_c, got, mine)], axis=1)
    return whole.reshape((8, 2) + array.shape[2:])


def head_lanes(head):
    lanes = lax.broadcasted_iota(jnp.int32, (1, 128), 1)
    return (lanes // 64) == head


def attend_kernel(q_ref, k_ref, v_ref, space_ref, time_ref, o_ref, p_ref):
    q, k, v = q_ref[...], k_ref[...], v_ref[...]
    rows = q.shape[0]
    total = jnp.zeros((rows, 128), f32)
    for head in range(2):
        lanes = head_lanes(head)
        scaled = jnp.where(lanes, q * jnp.asarray(0.125, bf16), jnp.zeros_like(q))
        scores = lax.dot_general(scaled, k, (((1,), (1,)), ((), ())), preferred_element_type=f32)
        shaped = scores.reshape(rows // SPATIAL, SPATIAL, rows)
        shaped = shaped + space_ref[head][None] + time_ref[0, head, : rows // SPATIAL][:, None, :]
        scores = shaped.reshape(rows, rows)
        grown = jnp.exp(scores - jnp.max(scores, axis=-1, keepdims=True))
        inverse = 1.0 / jnp.sum(grown, axis=-1, keepdims=True)
        probs = (grown * inverse).astype(bf16)
        p_ref[0, head] = probs
        masked = jnp.where(lanes, v, jnp.zeros_like(v))
        total = total + jnp.dot(probs, masked, preferred_element_type=f32)
    o_ref[...] = total.astype(bf16)


def attend_back_kernel(
    q_ref, k_ref, v_ref, do_ref, o_ref, p_ref, grad_ref, space_ref, time_ref
):
    q, k, v, do = q_ref[...], k_ref[...], v_ref[...], do_ref[...]
    rows = q.shape[0]
    slots = rows // SPATIAL
    product = do.astype(f32) * o_ref[...].astype(f32)
    grad_q = jnp.zeros((rows, 128), f32)
    grad_k = jnp.zeros((rows, 128), f32)
    grad_v = jnp.zeros((rows, 128), f32)

    @pl.when(pl.program_id(1) == 0)
    def _():
        space_ref[...] = jnp.zeros_like(space_ref)

    for head in range(2):
        lanes = head_lanes(head)
        none = jnp.zeros_like(q)
        scale = jnp.asarray(0.125, bf16)
        row_dot = jnp.sum(jnp.where(lanes, product, 0.0), axis=-1, keepdims=True)
        grads = jnp.where(lanes, do, none)
        probs = p_ref[0, head]
        grad_probs = lax.dot_general(
            grads, v, (((1,), (1,)), ((), ())), preferred_element_type=f32
        )
        grad_scores = probs.astype(f32) * (grad_probs - row_dot)
        low = grad_scores.astype(bf16)
        over_rows = (((0,), (0,)), ((), ()))
        grad_v = grad_v + lax.dot_general(probs, grads, over_rows, preferred_element_type=f32)
        grad_k = grad_k + lax.dot_general(
            low, jnp.where(lanes, q * scale, none), over_rows, preferred_element_type=f32
        )
        grad_q = grad_q + jnp.dot(
            low, jnp.where(lanes, k * scale, none), preferred_element_type=f32
        )
        shaped = grad_scores.reshape(slots, SPATIAL, rows)
        space_ref[head] += jnp.sum(shaped, axis=0)
        time_ref[0, head, :slots] = jnp.sum(shaped, axis=1)
    grad_ref[0] = grad_q.astype(bf16)
    grad_ref[1] = grad_k.astype(bf16)
    grad_ref[2] = grad_v.astype(bf16)


def attention_specs(rows, pairs):
    q_spec = pl.BlockSpec((rows, 128), lambda pair, window: (window, pair))
    k_spec = pl.BlockSpec((rows, 128), lambda pair, window: (window, pair + pairs))
    v_spec = pl.BlockSpec((rows, 128), lambda pair, window: (window, pair + 2 * pairs))
    p_spec = pl.BlockSpec((1, 2, rows, rows), lambda pair, window: (window, pair, 0, 0))
    space_spec = pl.BlockSpec((2, SPATIAL, rows), lambda pair, window: (pair, 0, 0))
    time_spec = pl.BlockSpec((1, 2, 8, rows), lambda pair, window: (window, pair, 0, 0))
    return q_spec, k_spec, v_spec, p_spec, space_spec, time_spec


def attend(projected, space_bias, time_bias, windows):
    rows = projected.shape[0] // windows
    heads = space_bias.shape[0]
    q_spec, k_spec, v_spec, p_spec, space_spec, time_spec = attention_specs(rows, heads // 2)
    width = heads * 64
    return pl.pallas_call(
        attend_kernel,
        grid=(heads // 2, windows),
        in_specs=[q_spec, k_spec, v_spec, space_spec, time_spec],
        out_specs=[q_spec, p_spec],
        out_shape=[
            jax.ShapeDtypeStruct((windows * rows, width), bf16),
            jax.ShapeDtypeStruct((windows, heads, rows, rows), bf16),
        ],
        compiler_params=pltpu.CompilerParams(vmem_limit_bytes=VMEM_LIMIT),
        cost_estimate=pl.CostEstimate(
            flops=16 * windows * heads * rows * rows * 64,
            bytes_accessed=windows * heads * rows * rows * 2,
            transcendentals=windows * heads * rows * rows,
        ),
        name="attend",
    )(projected, projected, projected, space_bias, time_bias)


def attend_back(projected, grad_attended, attended, probs, windows):
    heads, rows = probs.shape[1], probs.shape[2]
    q_spec, k_spec, v_spec, p_spec, space_spec, time_spec = attention_specs(rows, heads // 2)
    width = heads * 64
    return pl.pallas_call(
        attend_back_kernel,
        grid=(heads // 2, windows),
        in_specs=[q_spec, k_spec, v_spec, q_spec, q_spec, p_spec],
        out_specs=[
            pl.BlockSpec((3, rows, 128), lambda pair, window: (0, window, pair)),
            space_spec,
            time_spec,
        ],
        out_shape=[
            jax.ShapeDtypeStruct((3, windows * rows, width), bf16),
            jax.ShapeDtypeStruct((heads, SPATIAL, rows), f32),
            jax.ShapeDtypeStruct((windows, heads, 8, rows), f32),
        ],
        compiler_params=pltpu.CompilerParams(vmem_limit_bytes=VMEM_LIMIT),
        cost_estimate=pl.CostEstimate(
            flops=40 * windows * heads * rows * rows * 64,
            bytes_accessed=windows * heads * rows * rows * 2,
            transcendentals=0,
        ),
        name="attend_back",
    )(projected, projected, projected, grad_attended, attended, probs)


def normalize(values_in):
    centred = values_in - jnp.mean(values_in, axis=-1, keepdims=True)
    inverse = lax.rsqrt(jnp.mean(centred * centred, axis=-1, keepdims=True) + EPS)
    return centred * inverse, inverse


def normalize_back(grad_normed, normed, inverse):
    return inverse * (
        grad_normed
        - jnp.mean(grad_normed, axis=-1, keepdims=True)
        - normed * jnp.mean(grad_normed * normed, axis=-1, keepdims=True)
    )


def space_onehot():
    places = jnp.arange(SPATIAL, dtype=jnp.int32)
    across, along = places // SIDE, places % SIDE
    index = (across[:, None] - across[None, :] + SIDE - 1) * (2 * SIDE - 1) + (
        along[:, None] - along[None, :] + SIDE - 1
    )
    ids = jnp.arange((2 * SIDE - 1) ** 2, dtype=jnp.int32)
    return (index.reshape(-1)[:, None] == ids[None, :]).astype(f32)


def dot32(left, right, dims):
    return lax.dot_general(left, right, (dims, ((), ())), preferred_element_type=f32)


def on_device(
    tokens,
    condition,
    doubled,
    window_count,
    w_ada,
    b_ada,
    w_qkv,
    w_out,
    w_up,
    b_up,
    w_down,
    b_down,
    table_space,
    table_time,
    cotangent,
):
    windows, _, width = tokens.shape
    heads = table_space.shape[0]
    n_win = lax.axis_size("win")
    devices = n_win * 4
    win = lax.axis_index("win")
    frm = lax.axis_index("frm")
    z, x, y, c = win // 2, win % 2, frm // 2, frm % 2
    where = jnp.stack([z, x, y, c]).astype(jnp.int32)
    local = windows // 4
    ff = w_up.shape[1]
    ff_block = ff // devices
    shard_rows = w_qkv.shape[0]

    split_ff = pick(w_up.reshape(shard_rows, n_win * 2, 2, ff_block), c, 2)
    up_shard = split_ff.reshape(shard_rows, ff // 2)
    down_shard = pick(w_down.reshape(2, 2, ff_block, width), c, 1).reshape(2 * ff_block, width)
    attn_shard = pick(
        jnp.concatenate([w_qkv, w_out], axis=1).reshape(2, shard_rows // 2, 4 * width), c, 0
    )

    token_rows = windows_in(tokens, doubled, y, c)
    own_columns = b_ada.shape[0], b_up.shape[0], b_down.shape[0]
    small = jnp.concatenate([condition.reshape(-1), b_ada, b_up, b_down])
    small_all = lax.all_to_all(
        jnp.broadcast_to(small[None], (n_win, small.shape[0])),
        "win",
        split_axis=0,
        concat_axis=0,
        tiled=True,
    )
    attn_full = gather_weight(attn_shard, where, True).reshape(width, 4 * width)
    up_full = gather_weight(up_shard, where, False).reshape(width, ff // 2)
    down_full = gather_weight(down_shard, where, False).reshape(ff // 2, width)

    cond_size = windows * width
    cond_all = small_all[:, :cond_size].reshape(n_win * windows, width).astype(f32)
    cuts = [cond_size, cond_size + own_columns[0], cond_size + own_columns[0] + own_columns[1]]
    ada_bias = small_all[:, cuts[0] : cuts[1]].reshape(-1).astype(f32)
    up_bias = small_all[:, cuts[1] : cuts[2]].reshape(n_win * 2, 2, ff_block)
    up_bias = pick(up_bias, c, 1).reshape(-1).astype(f32)
    down_bias = small_all[:, cuts[2] :].reshape(-1).astype(f32)

    silu_all = jax.nn.silu(cond_all).astype(bf16)
    silu_part = lax.dynamic_slice_in_dim(silu_all, win * shard_rows, shard_rows, 1)
    ada_block = w_ada.shape[1] // devices
    ada_part = pick(w_ada.reshape(shard_rows, n_win, 4, ada_block), frm, 2)
    ada_part = ada_part.reshape(shard_rows, n_win * ada_block)
    mod_part = dot32(silu_part, ada_part, ((1,), (0,)))
    mod_parts = exchange_all(mod_part.reshape(devices, local, n_win * ada_block))
    modulation = jnp.sum(mod_parts.reshape(n_win, 4, local, n_win, ada_block), axis=0)
    modulation = jnp.transpose(modulation, (1, 2, 0, 3)).reshape(local, 6 * width) + ada_bias
    shift_one, scale_one, gate_one, shift_two, scale_two, gate_two = (
        block[:, None, :] for block in jnp.split(modulation, 6, axis=-1)
    )
    my_window = frm * local + jnp.arange(local, dtype=jnp.int32)
    live = (my_window < window_count[0]).astype(f32)[:, None, None]
    gate_one = gate_one * live
    gate_two = gate_two * live

    onehot_space = space_onehot()
    space_bias = jnp.dot(table_space, onehot_space.T, precision=exact_mode)
    space_bias = jnp.tile(space_bias.reshape(heads, SPATIAL, SPATIAL), (1, 1, FRAMES))
    mine_doubled = lax.dynamic_slice_in_dim(doubled, frm * local, local, 0)
    holders = jnp.arange(4, dtype=jnp.int32)
    frames = holders[None, :] + (holders[None, :] > mine_doubled[:, None]).astype(jnp.int32)
    frames = jnp.concatenate([frames, mine_doubled[:, None] + 1], axis=1)
    offset = frames[:, :, None] - frames[:, None, :] + FRAMES - 1
    onehot_time = (
        offset[..., None] == jnp.arange(table_time.shape[1], dtype=jnp.int32)
    ).astype(f32)
    time_bias = jnp.einsum("wabt,ht->whab", onehot_time, table_time, precision=exact_mode)
    time_bias = jnp.repeat(time_bias, SPATIAL, axis=-1)
    time_bias = jnp.pad(time_bias, ((0, 0), (0, 0), (0, 8 - FRAMES), (0, 0)))

    rows = FRAMES * SPATIAL
    token_full = token_rows.reshape(local, rows, width).astype(f32)
    normed_one, inverse_one = normalize(token_full)
    hidden_one = (normed_one * (1.0 + scale_one) + shift_one).astype(bf16)
    hidden_one = hidden_one.reshape(local * rows, width)
    qkv_full, out_full = attn_full[:, : 3 * width], attn_full[:, 3 * width :]
    projected = dot32(hidden_one, qkv_full, ((1,), (0,))).astype(bf16)
    attended, probs = attend(projected, space_bias, time_bias, local)
    branch_attn = dot32(attended, out_full, ((1,), (0,))).reshape(local, rows, width)
    mid = token_full + gate_one * branch_attn
    normed_two, inverse_two = normalize(mid)
    hidden_two = (normed_two * (1.0 + scale_two) + shift_two).astype(bf16)
    hidden_two = hidden_two.reshape(local * rows, width)

    grad_out = windows_in(cotangent, doubled, y, c).reshape(local, rows, width).astype(f32)
    grad_mlp = (gate_two * grad_out).astype(bf16).reshape(local * rows, width)
    hidden_both = jnp.concatenate([hidden_two, swap_core(hidden_two)])
    mlp_both = jnp.concatenate([grad_mlp, swap_core(grad_mlp)])
    pre_act = dot32(hidden_both, up_full, ((1,), (0,))) + up_bias
    activated = jax.nn.gelu(pre_act).astype(bf16)
    grad_down_w = dot32(activated, mlp_both, ((0,), (0,))).astype(bf16)
    down_grad = scatter_sum(grad_down_w.reshape(n_win, 2, ff_block, width), where)
    grad_activated = dot32(mlp_both, down_full, ((1,), (1,)))
    _, gelu_back = jax.vjp(jax.nn.gelu, pre_act)
    grad_pre = gelu_back(grad_activated)[0].astype(bf16)
    grad_up_w = dot32(grad_pre, hidden_both, ((0,), (0,))).astype(bf16)
    up_grad = scatter_sum(grad_up_w.reshape(n_win, 2, ff_block, width), where)
    grad_hidden_both = dot32(grad_pre, up_full, ((1,), (1,)))
    count = local * rows
    grad_hidden_two = (
        grad_hidden_both[:count]
        + swap_core(grad_hidden_both[count:].astype(bf16)).astype(f32)
    ).reshape(local, rows, width)
    mlp_part = dot32(activated, down_full, ((1,), (0,)))
    branch_mlp = mlp_part[:count] + swap_core(mlp_part[count:].astype(bf16)).astype(f32)
    branch_mlp = (branch_mlp + down_bias).reshape(local, rows, width)
    result = (mid + gate_two * branch_mlp).astype(bf16)
    result_back = windows_out(result.reshape(local, FRAMES, SPATIAL, width), y, c)

    grad_mid = grad_out + normalize_back(
        grad_hidden_two * (1.0 + scale_two), normed_two, inverse_two
    )
    grad_branch = (gate_one * grad_mid).astype(bf16).reshape(count, width)
    grad_attended = dot32(grad_branch, out_full, ((1,), (1,))).astype(bf16)
    grad_out_w = dot32(grad_branch, attended, ((0,), (0,))).astype(bf16)
    grad_projected, space_sums, time_sums = attend_back(
        projected, grad_attended, attended, probs, local
    )
    grad_qkv_w = lax.dot_general(
        grad_projected, hidden_one, (((1,), (0,)), ((), ())), preferred_element_type=f32
    ).astype(bf16)
    qkv_block, out_block = 3 * width // devices, width // devices
    grad_attn_w = jnp.concatenate(
        [
            grad_qkv_w.reshape(n_win, 2, 2, qkv_block, width),
            grad_out_w.reshape(n_win, 2, 2, out_block, width),
        ],
        axis=3,
    )
    attn_own = pick(grad_attn_w, c, 2)
    attn_other = swap_core(pick(grad_attn_w, 1 - c, 2))
    attn_grad = scatter_sum(add_low(attn_own, attn_other), where)
    grad_hidden_one = lax.dot_general(
        grad_projected[0], qkv_full[:, :width], (((1,), (1,)), ((), ())), preferred_element_type=f32
    )
    for part in (1, 2):
        grad_hidden_one = grad_hidden_one + dot32(
            grad_projected[part], qkv_full[:, part * width : (part + 1) * width], ((1,), (1,))
        )
    grad_hidden_one = grad_hidden_one.reshape(local, rows, width)
    grad_tokens = grad_mid + normalize_back(
        grad_hidden_one * (1.0 + scale_one), normed_one, inverse_one
    )
    tokens_back = windows_out(
        grad_tokens.astype(bf16).reshape(local, FRAMES, SPATIAL, width), y, c
    )

    row_live = jnp.stack([jnp.ones_like(doubled, dtype=bool), doubled == frm], axis=1)
    window_live = jnp.arange(windows, dtype=jnp.int32) < window_count[0]
    row_live = (row_live & window_live[:, None])[:, :, None, None]
    slots = (windows, 2, SPATIAL, width)
    result = jnp.where(row_live, result_back, tokens.reshape(slots)).reshape(tokens.shape)
    grad_tokens = jnp.where(
        row_live, tokens_back.astype(f32), cotangent.reshape(slots).astype(f32)
    ).reshape(tokens.shape)

    grad_mod = jnp.concatenate(
        [
            jnp.sum(grad_hidden_one, axis=1),
            jnp.sum(grad_hidden_one * normed_one, axis=1),
            jnp.sum(live * branch_attn * grad_mid, axis=1),
            jnp.sum(grad_hidden_two, axis=1),
            jnp.sum(grad_hidden_two * normed_two, axis=1),
            jnp.sum(live * branch_mlp * grad_out, axis=1),
        ],
        axis=-1,
    ).astype(bf16)
    mod_send = jnp.transpose(grad_mod.reshape(local, n_win, 4, ada_block), (2, 0, 1, 3))
    mod_send = jnp.broadcast_to(mod_send[None], (n_win, 4, local, n_win, ada_block))
    mod_got = exchange_all(mod_send.reshape(devices, local, n_win * ada_block))
    mod_got = mod_got.reshape(n_win * windows, n_win * ada_block)
    mod_own = lax.dynamic_slice_in_dim(mod_got, win * ada_block, ada_block, 1)
    grad_ada_w = dot32(silu_all, mod_own, ((0,), (0,)))
    grad_ada_b = jnp.sum(mod_own.astype(f32), axis=0)
    cond_part = dot32(mod_got, ada_part, ((1,), (1,)))

    grad_up_b = jnp.sum(grad_pre.astype(f32), axis=0).reshape(n_win * 2, 1, ff_block)
    core_mask = (jnp.arange(2, dtype=jnp.int32) == c).astype(f32)[None, :, None]
    grad_up_b = (grad_up_b * core_mask).reshape(devices, ff_block)
    grad_down_b = jnp.sum(grad_mlp.astype(f32), axis=0).reshape(devices, width // devices)
    space_sum = jnp.sum(space_sums.reshape(heads, SPATIAL, FRAMES, SPATIAL), axis=2)
    space_sum = jnp.dot(
        space_sum.reshape(heads, SPATIAL * SPATIAL), onehot_space, precision=exact_mode
    )
    time_sum = jnp.sum(
        time_sums[:, :, :FRAMES].reshape(local, heads, FRAMES, FRAMES, SPATIAL), axis=-1
    )
    time_sum = jnp.einsum("whab,wabt->ht", time_sum, onehot_time, precision=exact_mode)
    tables = jnp.concatenate([space_sum.reshape(-1), time_sum.reshape(-1)])
    share = -(-tables.shape[0] // devices)
    tables = jnp.pad(tables, (0, share * devices - tables.shape[0])).reshape(devices, share)
    sums = jnp.concatenate([grad_up_b, grad_down_b, tables], axis=1)
    sums = jnp.sum(exchange_all(sums), axis=0)
    out_up_b = sums[:ff_block]
    out_down_b = sums[ff_block : ff_block + width // devices]
    table_share = sums[ff_block + width // devices :]

    cond_send = cond_part.reshape(n_win, 1, windows * shard_rows)
    cond_send = jnp.broadcast_to(cond_send, (n_win, 4, windows * shard_rows))
    cond_send = cond_send.reshape(devices, windows * shard_rows)
    last_send = jnp.concatenate(
        [cond_send, jnp.broadcast_to(table_share[None], (devices, share))], axis=1
    )
    last_got = exchange_all(last_send)
    cond_grad = last_got[:, : windows * shard_rows].reshape(n_win, 4, windows, shard_rows)
    cond_grad = jnp.transpose(jnp.sum(cond_grad, axis=1), (1, 0, 2)).reshape(windows, width)
    _, silu_back = jax.vjp(jax.nn.silu, condition.astype(f32))
    grad_condition = silu_back(cond_grad)[0]
    table_all = last_got[:, windows * shard_rows :].reshape(-1)
    space_size = table_space.size
    grad_space = table_all[:space_size].reshape(table_space.shape)
    grad_time = table_all[space_size : space_size + table_time.size].reshape(table_time.shape)

    return (
        result,
        grad_tokens,
        grad_condition,
        grad_ada_w,
        grad_ada_b,
        attn_grad[:qkv_block].T,
        attn_grad[qkv_block:].T,
        up_grad.T,
        out_up_b,
        down_grad,
        out_down_b,
        grad_space,
        grad_time,
    )


def solution(mesh):
    return jax.shard_map(
        on_device,
        mesh=mesh,
        in_specs=(
            P("win", "frm", None),
            P("win", None),
            P("win"),
            P("win"),
            P("win", None),
            P("win"),
            P("win", None),
            P("win", None),
            P("win", None),
            P("win"),
            P("win", None),
            P("win"),
            P(),
            P(),
            P("win", "frm", None),
        ),
        out_specs=(
            P("win", "frm", None),
            P("win", "frm", None),
            P("win", None),
            P(None, BOTH),
            P(BOTH),
            P(None, BOTH),
            P(None, BOTH),
            P(None, BOTH),
            P(BOTH),
            P(BOTH, None),
            P(BOTH),
            P(),
            P(),
        ),
        check_vma=False,
    )
```

time: 2230 us -> 1150 us (0.52)
  waiting for transfers between devices: 1010 us -> 163 us
  Pallas kernels: 0 us -> 551 us
  local copies, waits for them, and re-layouts: 566 us -> 99.2 us
  matrix products: 379 us -> 115 us
  blocking collectives: 134 us -> 0 us
  starting transfers between devices: 0.52 us -> 96.5 us
    reduce_scatter x5 -> x0, waiting for transfers between devices: 640 us -> none  [the longest x1 252 us: on_device(): lax.psum_scatter(weight_grads[0], ('win', 'frm'), scatter_dimension=1, ti...]
    pallas_call x0 -> x5, Pallas kernels: none -> 551 us  [the longest x3 515 us: place(): pl.pallas_call(place_kernel, out_shape=jax.ShapeDtypeStruct(shape, near_a...]
    all_gather x8 -> x0, waiting for transfers between devices: 362 us -> none  [the longest x1 151 us: on_device(): lax.all_gather(weight_set[0], 'win', axis=0, tiled=True)]
    add x31 -> x2, local copies, waits for them, and re-layouts: 325 us -> 0.17 us  [the longest x1 0.1 us: on_device(): frames = jnp.concatenate([frames, mine_doubled[:, None] + 1], axis=1)]
    dot_general x41 -> x21, matrix products: 379 us -> 115 us  [the longest x15 99 us: dot32(): lax.dot_general(left, right, (dims, ((), ())), preferred_element_type=f32)]
    ppermute x0 -> x59, waiting for transfers between devices: none -> 163 us  [the longest x29 83.2 us: swap_frm(): return lax.ppermute(array, 'frm', [(j, j ^ bit) for j in range(4)])]
    all_gather x5 -> x0, blocking collectives: 74.7 us -> none  [the longest x1 22.9 us: on_device(): lax.all_gather(weight_set[1], 'win', axis=0, tiled=True)]
    ppermute x0 -> x59, starting transfers between devices: none -> 65.3 us  [the longest x29 35 us: swap_frm(): return lax.ppermute(array, 'frm', [(j, j ^ bit) for j in range(4)])]
  transfers between devices with their start and end apart: 13 -> 64, of which waited for: 8 -> 13; matrix products, arithmetic and copies ran while one was open for 42% -> 23% of each run, Pallas kernels for 0% -> 48%
where the time goes in v1:
time: 1150 us; the launch traced here: 1140 us
  Pallas kernels  551 us (48%)
  waiting for transfers between devices  163 us (14%)
  matrix products  115 us (10%)
  other arithmetic  110 us (10%)
  local copies, waits for them, and re-layouts  99.2 us (9%)
  starting transfers between devices  96.5 us (8%)
    pallas_call x3, Pallas kernels, place(): pl.pallas_call(place_kernel, out_shape=jax.ShapeDtypeStruct(shape, near_a...  515 us
    dot_general x15, matrix products, dot32(): lax.dot_general(left, right, (dims, ((), ())), preferred_element_type=f32)  99 us
    ppermute x29, waiting for transfers between devices, swap_frm(): return lax.ppermute(array, 'frm', [(j, j ^ bit) for j in range(4)])  83.2 us
    ppermute x30, waiting for transfers between devices, swap_win(): return lax.ppermute(array, 'win', [(j, j ^ bits) for j in range(count)])  79.7 us
    ppermute x29, starting transfers between devices, swap_frm(): return lax.ppermute(array, 'frm', [(j, j ^ bit) for j in range(4)])  35 us
    ppermute x30, starting transfers between devices, swap_win(): return lax.ppermute(array, 'win', [(j, j ^ bits) for j in range(count)])  30.3 us
    all_to_all x4, starting transfers between devices, exchange_all(): return lax.all_to_all(array, BOTH, split_axis=0, concat_axis=0, tiled=True)  25.5 us
  transfers between devices with their start and end apart: 64, of which 13 were waited for; matrix products, arithmetic and copies ran while one was open for 23% of the time, Pallas kernels for 48%

profile of v1, /device:TPU:9, one launch (start us, length us, event | category | flops | bytes accessed | tf_op | source)
XLA Modules:
  0.0 1139.0 jit_solution(10793582525242253612)
XLA Ops:
  13.6 5.7 all-to-all-start
  26.6 3.1 dynamic-slice_reduce_fusion
  35.3 3.3 dynamic-slice_bitcast_fusion.1
  64.2 7.2 collective-permute-start.31
  95.2 8.2 all-to-all-start.1
  114.8 9.5 collective-permute-done.19
  135.2 39.6 %collective-permute-done.1 = bf16[2,3,64,1024]{3,2,1,0:T(8,128)(2,1)S(1)} collective-permute-done((bf16[2,3,64,1024]{3,2,1,0:T(8,128)(2,1)S(1)}, bf16[2,3,64,1024]{3,2,1,0:T(8,128)(2,1)S(1)}, u32[]{:S(2)}, u32[]{:S(2)}) %collective-permute-start.1) | collective-permute-done | bytes 786464 | tf_op jit(solution)/shard_map/ppermute | solution.py:23
  185.4 256.5 %place.3 = bf16[8,2,2,32,4096]{4,3,2,1,0:T(8,128)(2,1)} custom-call(s32[4]{0:T(128)} %pad_add_fusion.1.where, bf16[2,4,32,1536]{3,2,1,0:T(8,128)(2,1)} %pad_maximum_fusion.25.refs_0_, bf16[2,4,32,1536]{3,2,1,0:T(8,128)(2,1)} %collective-permute-done.6.refs_1_, bf16[2,4,32,2560]{3,2,1,0:T(8,128)(2,1)} %pad_maximum_fusion.12.refs_2_, ...), custom_call_target="tpu_custom_call" | custom-call | bytes 3145728 | tf_op jit(solution)/shard_map/place/pallas_call | solution.py:86
  442.0 9.3 fusion.10.q_ref.k_ref.v_ref
  451.3 17.0 %attend.1 = (bf16[640,1024]{1,0:T(8,128)(2,1)S(1)}, bf16[2,16,320,320]{3,2,1,0:T(8,128)(2,1)}) custom-call(bf16[640,3072]{1,0:T(8,128)(2,1)} %fusion.10.q_ref.k_ref.v_ref, bf16[640,3072]{1,0:T(8,128)(2,1)} %fusion.10.q_ref.k_ref.v_ref, bf16[640,3072]{1,0:T(8,128)(2,1)} %fusion.10.q_ref.k_ref.v_ref, f32[16,64,320]{2,1,0:T(8,128)S(1)} %copy.175.space_ref, ...), custom_call_target="tpu_custom_call" | custom-call | flops 3355443200 | bytes 6553600 | tf_op jit(solution)/shard_map/attend/pallas_call | solution.py:281
  468.3 3.2 fusion.69
  488.3 25.4 %collective-permute-done.18.refs_1_ = bf16[2,4,64,768]{3,2,1,0:T(8,128)(2,1)} collective-permute-done((bf16[2,4,64,768]{3,2,1,0:T(8,128)(2,1)}, bf16[2,4,64,768]{3,2,1,0:T(8,128)(2,1)}, u32[]{:S(2)}, u32[]{:S(2)}) %collective-permute-start.18) | collective-permute-done | bytes 786464 | tf_op jit(solution)/shard_map/ppermute | solution.py:23
  514.5 129.1 %place.4 = bf16[8,2,64,2048]{3,2,1,0:T(8,128)(2,1)} custom-call(s32[4]{0:T(128)} %pad_add_fusion.1.where, bf16[2,4,64,768]{3,2,1,0:T(8,128)(2,1)} %pad_maximum_fusion.26.refs_0_, bf16[2,4,64,768]{3,2,1,0:T(8,128)(2,1)} %collective-permute-done.18.refs_1_, bf16[2,4,64,1280]{3,2,1,0:T(8,128)(2,1)} %pad_maximum_fusion.13.refs_2_, ...), custom_call_target="tpu_custom_call" | custom-call | bytes 3145728 | tf_op jit(solution)/shard_map/place/pallas_call | solution.py:86
  643.7 129.1 %place.5 = bf16[8,2,128,1024]{3,2,1,0:T(8,128)(2,1)} custom-call(s32[4]{0:T(128)} %pad_add_fusion.1.where, bf16[2,4,128,384]{3,2,1,0:T(8,128)(2,1)} %copy-done.36, bf16[2,4,128,384]{3,2,1,0:T(8,128)(2,1)} %collective-permute-done.25.refs_1_, bf16[2,4,128,640]{3,2,1,0:T(8,128)(2,1)} %pad_maximum_fusion.14.refs_2_, ...), custom_call_target="tpu_custom_call" | custom-call | bytes 3145728 | tf_op jit(solution)/shard_map/place/pallas_call | solution.py:86
  775.5 12.8 %multiply_convert_fusion = (bf16[1280,2048]{1,0:T(8,128)(2,1)S(1)}, f32[1280,2048]{1,0:T(8,128)}) fusion(f32[2048]{0:T(1024)S(1)} %bitcast.562, bf16[1024,2048]{1,0:T(8,128)(2,1)} %bitcast.531, bf16[640,1024]{1,0:T(8,128)(2,1)} %collective-permute-done.13, bf16[640,1024]{1,0:T(8,128)(2,1)} %fusion.25), kind=kOutput, calls=%fused_computation.12 | convolution fusion | flops 5400166400 | bytes 22552576 | tf_op jit(solution)/shard_map/dot_general | solution.py:353
  788.3 18.8 %convert_reduce_fusion = (f32[2048]{0:T(1024)S(1)}, bf16[1280,2048]{1,0:T(8,128)(2,1)}) fusion(f32[1280,2048]{1,0:T(8,128)} %get-tuple-element.113, f32[2048]{0:T(1024)S(1)} %bitcast.563, bf16[2048,1024]{1,0:T(8,128)(2,1)S(1)} %bitcast.533, bf16[640,1024]{1,0:T(8,128)(2,1)} %collective-permute-done.33, bf16[640,1024]{1,0:T(8,128)(2,1)} %fusion.44), kind=kOutput, calls=%fused_computation.11 | convolution fusion | flops 5434243072 | bytes 22560768 | tf_op jit(solution)/shard_map/dot_general | solution.py:353
  807.2 9.5 fusion.168
  816.6 7.7 convolution_convert_fusion.1
  826.0 7.7 fusion.167
  839.9 8.8 convolution_convert_fusion
  851.0 3.7 slice.540
  861.4 3.1 slice.541
  870.7 14.6 %collective-permute-done.52 = bf16[4,2,128,512]{3,2,0,1:T(8,128)(2,1)} collective-permute-done((bf16[4,2,128,512]{3,2,0,1:T(8,128)(2,1)}, bf16[4,2,128,512]{3,2,0,1:T(8,128)(2,1)}, u32[]{:S(2)}, u32[]{:S(2)}) %collective-permute-start.52) | collective-permute-done | bytes 1048608 | tf_op jit(solution)/shard_map/ppermute | solution.py:36
  892.4 4.8 fusion.50
  899.8 3.5 fusion.23
  903.2 3.2 convolution_convert_fusion.3
  906.4 3.2 fusion.70.do_ref
  915.3 19.7 %attend_back.1 = (bf16[3,640,1024]{2,1,0:T(8,128)(2,1)}, f32[16,64,320]{2,1,0:T(8,128)}, f32[2,16,8,320]{3,2,1,0:T(8,128)S(1)}) custom-call(bf16[640,3072]{1,0:T(8,128)(2,1)} %fusion.10.q_ref.k_ref.v_ref, bf16[640,3072]{1,0:T(8,128)(2,1)} %fusion.10.q_ref.k_ref.v_ref, bf16[640,3072]{1,0:T(8,128)(2,1)} %fusion.10.q_ref.k_ref.v_ref, ...), custom_call_target="tpu_custom_call" | custom-call | flops 8388608000 | bytes 6553600 | tf_op jit(solution)/shard_map/attend_back/pallas_call | solution.py:304
  935.0 5.3 fusion.53
  940.3 4.8 fusion.55
  945.1 7.1 convolution_convert_fusion.2
  953.0 3.3 copy.180
  965.6 4.0 all-to-all-start.3
  969.7 7.0 fusion.49
  980.7 3.3 multiply_reduce_fusion
  986.9 4.4 fusion.37
  998.5 5.7 all-to-all-start.2
  1018.1 7.5 all-to-all-start.4
  1029.7 5.1 collective-permute-done.51
  1038.3 15.5 %collective-permute-done.57 = bf16[128,1024]{1,0:T(8,128)(2,1)S(1)} collective-permute-done((bf16[128,1024]{1,0:T(8,128)(2,1)}, bf16[128,1024]{1,0:T(8,128)(2,1)S(1)}, u32[]{:S(2)}, u32[]{:S(2)}) %collective-permute-start.57) | collective-permute-done | bytes 262176 | tf_op jit(solution)/shard_map/ppermute | solution.py:36
  1053.8 6.6 collective-permute-done.58
  1068.0 4.9 collective-permute-start.36
  1073.0 3.7 fusion.7
  1081.8 18.4 %collective-permute-done.38 = bf16[4,2,128,512]{3,2,0,1:T(8,128)(2,1)S(1)} collective-permute-done((bf16[4,2,128,512]{3,2,0,1:T(8,128)(2,1)S(1)}, bf16[4,2,128,512]{3,2,0,1:T(8,128)(2,1)S(1)}, u32[]{:S(2)}, u32[]{:S(2)}) %collective-permute-start.38) | collective-permute-done | bytes 1048608 | tf_op jit(solution)/shard_map/ppermute | solution.py:36
  1105.1 7.1 collective-permute-done.39
  1112.9 3.0 collective-permute-start.43
  1119.2 5.2 collective-permute-done.43
  1124.4 12.6 %collective-permute-done.44 = bf16[128,1024]{1,0:T(8,128)(2,1)S(1)} collective-permute-done((bf16[128,1024]{1,0:T(8,128)(2,1)S(1)}, bf16[128,1024]{1,0:T(8,128)(2,1)S(1)}, u32[]{:S(2)}, u32[]{:S(2)}) %collective-permute-start.44) | collective-permute-done | bytes 262176 | tf_op jit(solution)/shard_map/ppermute | solution.py:36
  (589 shorter events, 233.2 us)
Async XLA Ops:
  2.6 59.5 %collective-permute-start.23 = (bf16[128,1024]{1,0:T(8,128)(2,1)}, bf16[128,1024]{1,0:T(8,128)(2,1)}, u32[]{:S(2)}, u32[]{:S(2)}) collective-permute-start(bf16[128,1024]{1,0:T(8,128)(2,1)} %dynamic-slice_bitcast_fusion.8), channel_id=1, source_target_pairs={{0,24},{4,28},{8,16},{12,20},{16,8},{20,12},{24,0},{28,4},{1,25},{... | collective-permute-start | bytes 786440 | tf_op jit(solution)/shard_map/ppermute | solution.py:36
  3.9 60.3 %collective-permute-start.22 = (bf16[128,1024]{1,0:T(8,128)(2,1)}, bf16[128,1024]{1,0:T(8,128)(2,1)}, u32[]{:S(2)}, u32[]{:S(2)}) collective-permute-start(bf16[128,1024]{1,0:T(8,128)(2,1)} %dynamic-slice_bitcast_fusion.8), channel_id=1, source_target_pairs={{0,16},{4,20},{8,24},{12,28},{16,0},{20,4},{24,8},{28,12},{1,17},{... | collective-permute-start | bytes 786440 | tf_op jit(solution)/shard_map/ppermute | solution.py:36
  4.9 68.4 %collective-permute-start.21 = (bf16[128,1024]{1,0:T(8,128)(2,1)}, bf16[128,1024]{1,0:T(8,128)(2,1)}, u32[]{:S(2)}, u32[]{:S(2)}) collective-permute-start(bf16[128,1024]{1,0:T(8,128)(2,1)} %dynamic-slice_bitcast_fusion.8), channel_id=1, source_target_pairs={{0,8},{4,12},{8,0},{12,4},{16,24},{20,28},{24,16},{28,20},{1,9},{5... | collective-permute-start | bytes 786440 | tf_op jit(solution)/shard_map/ppermute | solution.py:36
  8.2 44.2 %collective-permute-start.4 = (bf16[32,4096]{1,0:T(8,128)(2,1)}, bf16[32,4096]{1,0:T(8,128)(2,1)}, u32[]{:S(2)}, u32[]{:S(2)}) collective-permute-start(bf16[32,4096]{1,0:T(8,128)(2,1)} %dynamic-slice_bitcast_fusion.10), channel_id=1, source_target_pairs={{0,24},{4,28},{8,16},{12,20},{16,8},{20,12},{24,0},{28,4},{1,25},{... | collective-permute-start | bytes 786440 | tf_op jit(solution)/shard_map/ppermute | solution.py:36
  9.4 44.9 %collective-permute-start.3 = (bf16[32,4096]{1,0:T(8,128)(2,1)}, bf16[32,4096]{1,0:T(8,128)(2,1)}, u32[]{:S(2)}, u32[]{:S(2)}) collective-permute-start(bf16[32,4096]{1,0:T(8,128)(2,1)} %dynamic-slice_bitcast_fusion.10), channel_id=1, source_target_pairs={{0,16},{4,20},{8,24},{12,28},{16,0},{20,4},{24,8},{28,12},{1,17},{... | collective-permute-start | bytes 786440 | tf_op jit(solution)/shard_map/ppermute | solution.py:36
  13.6 69.8 %all-to-all-start = ((bf16[8,2,4800]{2,1,0:T(2,128)(2,1)}), bf16[8,2,4800]{2,1,0:T(2,128)(2,1)}, u32[]{:S(2)}, u32[]{:S(2)}) async-start(bf16[8,2,4800]{2,1,0:T(2,128)(2,1)} %reshape.757), calls=%async_computation | async-start | bytes 311296 | tf_op jit(solution)/shard_map/all_to_all | solution.py:396
  54.2 22.2 %collective-permute-start.16 = (bf16[64,2048]{1,0:T(8,128)(2,1)}, bf16[64,2048]{1,0:T(8,128)(2,1)S(1)}, u32[]{:S(2)}, u32[]{:S(2)}) collective-permute-start(bf16[64,2048]{1,0:T(8,128)(2,1)} %copy-done.51), channel_id=1, source_target_pairs={{0,24},{4,28},{8,16},{12,20},{16,8},{20,12},{24,0},{28,4},{1,25},{... | collective-permute-start | bytes 786440 | tf_op jit(solution)/shard_map/ppermute | solution.py:36
  64.2 64.8 %collective-permute-start.31 = (bf16[2,2,2,64,1024]{4,3,2,1,0:T(8,128)(2,1)}, bf16[2,2,2,64,1024]{4,3,2,1,0:T(8,128)(2,1)}, u32[]{:S(2)}, u32[]{:S(2)}) collective-permute-start(bf16[2,2,2,64,1024]{4,3,2,1,0:T(8,128)(2,1)} %get-tuple-element.53), channel_id=1, source_target_pairs={{0,1},{1,0},{2,3},{3,2},{4,5},{5,4},{6,7},{7,6},{8,9},{9,8},{10,11... | collective-permute-start | bytes 3145736 | tf_op jit(solution)/shard_map/ppermute | solution.py:23
  73.3 59.1 %collective-permute-start = (bf16[2,2,2,64,1024]{4,3,2,1,0:T(8,128)(2,1)}, bf16[2,2,2,64,1024]{4,3,2,1,0:T(8,128)(2,1)}, u32[]{:S(2)}, u32[]{:S(2)}) collective-permute-start(bf16[2,2,2,64,1024]{4,3,2,1,0:T(8,128)(2,1)} %get-tuple-element.58), channel_id=1, source_target_pairs={{0,1},{1,0},{2,3},{3,2},{4,5},{5,4},{6,7},{7,6},{8,9},{9,8},{10,11... | collective-permute-start | bytes 3145736 | tf_op jit(solution)/shard_map/ppermute | solution.py:23
  76.5 33.9 %collective-permute-start.26 = (bf16[4,128,640]{2,1,0:T(8,128)(2,1)}, bf16[4,128,640]{2,1,0:T(8,128)(2,1)}, u32[]{:S(2)}, u32[]{:S(2)}) collective-permute-start(bf16[4,128,640]{2,1,0:T(8,128)(2,1)} %get-tuple-element.89), channel_id=1, source_target_pairs={{0,2},{1,3},{2,0},{3,1},{4,6},{5,7},{6,4},{7,5},{8,10},{9,11},{10,... | collective-permute-start | bytes 1966088 | tf_op jit(solution)/shard_map/ppermute | solution.py:23
  78.8 24.6 %collective-permute-start.5 = (bf16[4,32,1536]{2,1,0:T(8,128)(2,1)}, bf16[4,32,1536]{2,1,0:T(8,128)(2,1)}, u32[]{:S(2)}, u32[]{:S(2)}) collective-permute-start(bf16[4,32,1536]{2,1,0:T(8,128)(2,1)} %get-tuple-element.97), channel_id=1, source_target_pairs={{0,4},{4,0},{8,12},{12,8},{16,20},{20,16},{24,28},{28,24},{1,5},{5... | collective-permute-start | bytes 1179656 | tf_op jit(solution)/shard_map/ppermute | solution.py:36
  81.0 25.7 %collective-permute-start.7 = (bf16[4,32,2560]{2,1,0:T(8,128)(2,1)}, bf16[4,32,2560]{2,1,0:T(8,128)(2,1)}, u32[]{:S(2)}, u32[]{:S(2)}) collective-permute-start(bf16[4,32,2560]{2,1,0:T(8,128)(2,1)} %get-tuple-element.91), channel_id=1, source_target_pairs={{0,2},{1,3},{2,0},{3,1},{4,6},{5,7},{6,4},{7,5},{8,10},{9,11},{10,... | collective-permute-start | bytes 1966088 | tf_op jit(solution)/shard_map/ppermute | solution.py:23
  95.2 31.5 %all-to-all-start.1 = ((f32[32,2,1536]{2,1,0:T(2,128)}), f32[32,2,1536]{2,1,0:T(2,128)S(1)}, u32[]{:S(2)}, u32[]{:S(2)}) async-start(f32[32,2,1536]{2,1,0:T(2,128)} %copy.166), calls=%async_computation.1 | async-start | bytes 786432 | tf_op jit(solution)/shard_map/all_to_all | solution.py:40
  103.4 20.9 %collective-permute-start.19 = (bf16[4,64,1280]{2,1,0:T(8,128)(2,1)}, bf16[4,64,1280]{2,1,0:T(8,128)(2,1)S(1)}, u32[]{:S(2)}, u32[]{:S(2)}) collective-permute-start(bf16[4,64,1280]{2,1,0:T(8,128)(2,1)} %get-tuple-element.93), channel_id=1, source_target_pairs={{0,2},{1,3},{2,0},{3,1},{4,6},{5,7},{6,4},{7,5},{8,10},{9,11},{10,... | collective-permute-start | bytes 1966088 | tf_op jit(solution)/shard_map/ppermute | solution.py:23
  106.7 369.7 %collective-permute-start.24 = (bf16[4,128,384]{2,1,0:T(8,128)(2,1)}, bf16[4,128,384]{2,1,0:T(8,128)(2,1)}, u32[]{:S(2)}, u32[]{:S(2)}) collective-permute-start(bf16[4,128,384]{2,1,0:T(8,128)(2,1)} %get-tuple-element.95), channel_id=1, source_target_pairs={{0,4},{4,0},{8,12},{12,8},{16,20},{20,16},{24,28},{28,24},{1,5},{5... | collective-permute-start | bytes 1179656 | tf_op jit(solution)/shard_map/ppermute | solution.py:36
  110.4 66.5 %collective-permute-start.6 = (bf16[2,4,32,1536]{3,2,1,0:T(8,128)(2,1)}, bf16[2,4,32,1536]{3,2,1,0:T(8,128)(2,1)}, u32[]{:S(2)}, u32[]{:S(2)}) collective-permute-start(bf16[2,4,32,1536]{3,2,1,0:T(8,128)(2,1)} %pad_maximum_fusion.25.refs_0_), channel_id=1, source_target_pairs={{0,2},{1,3},{2,0},{3,1},{4,6},{5,7},{6,4},{7,5},{8,10},{9,11},{10,... | collective-permute-start | bytes 2359304 | tf_op jit(solution)/shard_map/ppermute | solution.py:23
  124.3 52.5 %collective-permute-start.8 = (bf16[2,4,32,2560]{3,2,1,0:T(8,128)(2,1)}, bf16[2,4,32,2560]{3,2,1,0:T(8,128)(2,1)}, u32[]{:S(2)}, u32[]{:S(2)}) collective-permute-start(bf16[2,4,32,2560]{3,2,1,0:T(8,128)(2,1)} %pad_maximum_fusion.12.refs_2_), channel_id=1, source_target_pairs={{0,4},{4,0},{8,12},{12,8},{16,20},{20,16},{24,28},{28,24},{1,5},{5... | collective-permute-start | bytes 3932168 | tf_op jit(solution)/shard_map/ppermute | solution.py:36
  131.1 46.4 %collective-permute-start.32 = (bf16[2,3,64,1024]{3,2,1,0:T(8,128)(2,1)S(1)}, bf16[2,3,64,1024]{3,2,1,0:T(8,128)(2,1)S(1)}, u32[]{:S(2)}, u32[]{:S(2)}) collective-permute-start(bf16[2,3,64,1024]{3,2,1,0:T(8,128)(2,1)S(1)} %get-tuple-element.64), channel_id=1, source_target_pairs={{0,2},{1,3},{2,0},{3,1},{4,6},{5,7},{6,4},{7,5},{8,10},{9,11},{10,... | collective-permute-start | bytes 2359304 | tf_op jit(solution)/shard_map/ppermute | solution.py:23
  134.2 40.7 %collective-permute-start.1 = (bf16[2,3,64,1024]{3,2,1,0:T(8,128)(2,1)S(1)}, bf16[2,3,64,1024]{3,2,1,0:T(8,128)(2,1)S(1)}, u32[]{:S(2)}, u32[]{:S(2)}) collective-permute-start(bf16[2,3,64,1024]{3,2,1,0:T(8,128)(2,1)S(1)} %get-tuple-element.70), channel_id=1, source_target_pairs={{0,2},{1,3},{2,0},{3,1},{4,6},{5,7},{6,4},{7,5},{8,10},{9,11},{10,... | collective-permute-start | bytes 2359304 | tf_op jit(solution)/shard_map/ppermute | solution.py:23
  182.8 296.1 %collective-permute-start.17 = (bf16[4,64,768]{2,1,0:T(8,128)(2,1)}, bf16[4,64,768]{2,1,0:T(8,128)(2,1)}, u32[]{:S(2)}, u32[]{:S(2)}) collective-permute-start(bf16[4,64,768]{2,1,0:T(8,128)(2,1)} %get-tuple-element.99), channel_id=1, source_target_pairs={{0,4},{4,0},{8,12},{12,8},{16,20},{20,16},{24,28},{28,24},{1,5},{5... | collective-permute-start | bytes 1179656 | tf_op jit(solution)/shard_map/ppermute | solution.py:36
  184.0 330.6 %collective-permute-start.20 = (bf16[2,4,64,1280]{3,2,1,0:T(8,128)(2,1)}, bf16[2,4,64,1280]{3,2,1,0:T(8,128)(2,1)}, u32[]{:S(2)}, u32[]{:S(2)}) collective-permute-start(bf16[2,4,64,1280]{3,2,1,0:T(8,128)(2,1)} %pad_maximum_fusion.13.refs_2_), channel_id=1, source_target_pairs={{0,4},{4,0},{8,12},{12,8},{16,20},{20,16},{24,28},{28,24},{1,5},{5... | collective-permute-start | bytes 3932168 | tf_op jit(solution)/shard_map/ppermute | solution.py:36
  185.1 458.6 %collective-permute-start.27 = (bf16[2,4,128,640]{3,2,1,0:T(8,128)(2,1)}, bf16[2,4,128,640]{3,2,1,0:T(8,128)(2,1)}, u32[]{:S(2)}, u32[]{:S(2)}) collective-permute-start(bf16[2,4,128,640]{3,2,1,0:T(8,128)(2,1)} %pad_maximum_fusion.14.refs_2_), channel_id=1, source_target_pairs={{0,4},{4,0},{8,12},{12,8},{16,20},{20,16},{24,28},{28,24},{1,5},{5... | collective-permute-start | bytes 3932168 | tf_op jit(solution)/shard_map/ppermute | solution.py:36
  475.2 300.3 %collective-permute-start.13 = (bf16[640,1024]{1,0:T(8,128)(2,1)}, bf16[640,1024]{1,0:T(8,128)(2,1)}, u32[]{:S(2)}, u32[]{:S(2)}) collective-permute-start(bf16[640,1024]{1,0:T(8,128)(2,1)} %fusion.25), channel_id=1, source_target_pairs={{0,1},{1,0},{2,3},{3,2},{4,5},{5,4},{6,7},{7,6},{8,9},{9,8},{10,11... | collective-permute-start | bytes 3932168 | tf_op jit(solution)/shard_map/ppermute | solution.py:23
  477.5 166.1 %collective-permute-start.25 = (bf16[2,4,128,384]{3,2,1,0:T(8,128)(2,1)S(1)}, bf16[2,4,128,384]{3,2,1,0:T(8,128)(2,1)}, u32[]{:S(2)}, u32[]{:S(2)}) collective-permute-start(bf16[2,4,128,384]{3,2,1,0:T(8,128)(2,1)S(1)} %pad_maximum_fusion.27.refs_0_), channel_id=1, source_target_pairs={{0,2},{1,3},{2,0},{3,1},{4,6},{5,7},{6,4},{7,5},{8,10},{9,11},{10,... | collective-permute-start | bytes 2359304 | tf_op jit(solution)/shard_map/ppermute | solution.py:23
  480.9 32.9 %collective-permute-start.18 = (bf16[2,4,64,768]{3,2,1,0:T(8,128)(2,1)}, bf16[2,4,64,768]{3,2,1,0:T(8,128)(2,1)}, u32[]{:S(2)}, u32[]{:S(2)}) collective-permute-start(bf16[2,4,64,768]{3,2,1,0:T(8,128)(2,1)} %pad_maximum_fusion.26.refs_0_), channel_id=1, source_target_pairs={{0,2},{1,3},{2,0},{3,1},{4,6},{5,7},{6,4},{7,5},{8,10},{9,11},{10,... | collective-permute-start | bytes 2359304 | tf_op jit(solution)/shard_map/ppermute | solution.py:23
  513.7 274.6 %collective-permute-start.33 = (bf16[640,1024]{1,0:T(8,128)(2,1)}, bf16[640,1024]{1,0:T(8,128)(2,1)}, u32[]{:S(2)}, u32[]{:S(2)}) collective-permute-start(bf16[640,1024]{1,0:T(8,128)(2,1)} %fusion.44), channel_id=1, source_target_pairs={{0,1},{1,0},{2,3},{3,2},{4,5},{5,4},{6,7},{7,6},{8,9},{9,8},{10,11... | collective-permute-start | bytes 3932168 | tf_op jit(solution)/shard_map/ppermute | solution.py:23
  837.8 27.4 %collective-permute-start.45 = (bf16[4,2,128,512]{2,3,0,1:T(8,128)(2,1)}, bf16[4,2,128,512]{2,3,0,1:T(8,128)(2,1)}, u32[]{:S(2)}, u32[]{:S(2)}) collective-permute-start(bf16[4,2,128,512]{2,3,0,1:T(8,128)(2,1)} %bitcast.545), channel_id=1, source_target_pairs={{0,4},{4,0},{8,12},{12,8},{16,20},{20,16},{24,28},{28,24},{1,5},{5... | collective-permute-start | bytes 3145736 | tf_op jit(solution)/shard_map/ppermute | solution.py:36
  838.6 28.8 %collective-permute-start.47 = (bf16[4,2,128,512]{2,3,0,1:T(8,128)(2,1)}, bf16[4,2,128,512]{2,3,0,1:T(8,128)(2,1)}, u32[]{:S(2)}, u32[]{:S(2)}) collective-permute-start(bf16[4,2,128,512]{2,3,0,1:T(8,128)(2,1)} %bitcast.544), channel_id=1, source_target_pairs={{0,2},{1,3},{2,0},{3,1},{4,6},{5,7},{6,4},{7,5},{8,10},{9,11},{10,... | collective-permute-start | bytes 3145736 | tf_op jit(solution)/shard_map/ppermute | solution.py:23
  850.4 34.9 %collective-permute-start.52 = (bf16[4,2,128,512]{3,2,0,1:T(8,128)(2,1)}, bf16[4,2,128,512]{3,2,0,1:T(8,128)(2,1)}, u32[]{:S(2)}, u32[]{:S(2)}) collective-permute-start(bf16[4,2,128,512]{3,2,0,1:T(8,128)(2,1)} %copy_bitcast_fusion.1), channel_id=1, source_target_pairs={{0,4},{4,0},{8,12},{12,8},{16,20},{20,16},{24,28},{28,24},{1,5},{5... | collective-permute-start | bytes 3145736 | tf_op jit(solution)/shard_map/ppermute | solution.py:36
  854.8 37.0 %collective-permute-start.34 = (bf16[640,1024]{1,0:T(8,128)(2,1)}, bf16[640,1024]{1,0:T(8,128)(2,1)}, u32[]{:S(2)}, u32[]{:S(2)}) collective-permute-start(bf16[640,1024]{1,0:T(8,128)(2,1)} %slice.540), channel_id=1, source_target_pairs={{0,1},{1,0},{2,3},{3,2},{4,5},{5,4},{6,7},{7,6},{8,9},{9,8},{10,11... | collective-permute-start | bytes 3932168 | tf_op jit(solution)/shard_map/ppermute | solution.py:23
  856.4 31.9 %collective-permute-start.54 = (bf16[4,2,128,512]{3,2,0,1:T(8,128)(2,1)}, bf16[4,2,128,512]{3,2,0,1:T(8,128)(2,1)}, u32[]{:S(2)}, u32[]{:S(2)}) collective-permute-start(bf16[4,2,128,512]{3,2,0,1:T(8,128)(2,1)} %copy_bitcast_fusion), channel_id=1, source_target_pairs={{0,2},{1,3},{2,0},{3,1},{4,6},{5,7},{6,4},{7,5},{8,10},{9,11},{10,... | collective-permute-start | bytes 3145736 | tf_op jit(solution)/shard_map/ppermute | solution.py:23
  865.1 44.5 %collective-permute-start.28 = (bf16[640,1024]{1,0:T(8,128)(2,1)}, bf16[640,1024]{1,0:T(8,128)(2,1)}, u32[]{:S(2)}, u32[]{:S(2)}) collective-permute-start(bf16[640,1024]{1,0:T(8,128)(2,1)} %slice.541), channel_id=1, source_target_pairs={{0,1},{1,0},{2,3},{3,2},{4,5},{5,4},{6,7},{7,6},{8,9},{9,8},{10,11... | collective-permute-start | bytes 3932168 | tf_op jit(solution)/shard_map/ppermute | solution.py:23
  867.4 137.9 %collective-permute-start.46 = (bf16[4,128,512]{1,2,0:T(8,128)(2,1)}, bf16[4,128,512]{1,2,0:T(8,128)(2,1)}, u32[]{:S(2)}, u32[]{:S(2)}) collective-permute-start(bf16[4,128,512]{1,2,0:T(8,128)(2,1)} %fusion.95), channel_id=1, source_target_pairs={{0,2},{1,3},{2,0},{3,1},{4,6},{5,7},{6,4},{7,5},{8,10},{9,11},{10,... | collective-permute-start | bytes 1572872 | tf_op jit(solution)/shard_map/ppermute | solution.py:23
  885.3 121.4 %collective-permute-start.48 = (bf16[4,128,512]{1,2,0:T(8,128)(2,1)}, bf16[4,128,512]{1,2,0:T(8,128)(2,1)}, u32[]{:S(2)}, u32[]{:S(2)}) collective-permute-start(bf16[4,128,512]{1,2,0:T(8,128)(2,1)} %fusion.92), channel_id=1, source_target_pairs={{0,4},{4,0},{8,12},{12,8},{16,20},{20,16},{24,28},{28,24},{1,5},{5... | collective-permute-start | bytes 1572872 | tf_op jit(solution)/shard_map/ppermute | solution.py:36
  888.3 123.2 %collective-permute-start.53 = (bf16[4,128,512]{2,1,0:T(8,128)(2,1)}, bf16[4,128,512]{2,1,0:T(8,128)(2,1)}, u32[]{:S(2)}, u32[]{:S(2)}) collective-permute-start(bf16[4,128,512]{2,1,0:T(8,128)(2,1)} %fusion.89), channel_id=1, source_target_pairs={{0,2},{1,3},{2,0},{3,1},{4,6},{5,7},{6,4},{7,5},{8,10},{9,11},{10,... | collective-permute-start | bytes 1572872 | tf_op jit(solution)/shard_map/ppermute | solution.py:23
  891.7 121.6 %collective-permute-start.55 = (bf16[4,128,512]{2,1,0:T(8,128)(2,1)}, bf16[4,128,512]{2,1,0:T(8,128)(2,1)}, u32[]{:S(2)}, u32[]{:S(2)}) collective-permute-start(bf16[4,128,512]{2,1,0:T(8,128)(2,1)} %fusion.86), channel_id=1, source_target_pairs={{0,4},{4,0},{8,12},{12,8},{16,20},{20,16},{24,28},{28,24},{1,5},{5... | collective-permute-start | bytes 1572872 | tf_op jit(solution)/shard_map/ppermute | solution.py:36
  965.6 32.9 %all-to-all-start.3 = ((f32[32,1,277]{2,1,0:T(1,128)}), f32[32,1,277]{2,1,0:T(1,128)S(1)}, u32[]{:S(2)}, u32[]{:S(2)}) async-start(f32[32,1,277]{2,1,0:T(1,128)} %all_to_all.30), calls=%async_computation.3 | async-start | bytes 98304 | tf_op jit(solution)/shard_map/all_to_all | solution.py:40
  995.3 77.6 %collective-permute-start.37 = (bf16[8,2,128,1024]{3,2,1,0:T(8,128)(2,1)}, bf16[8,2,128,1024]{3,2,1,0:T(8,128)(2,1)}, u32[]{:S(2)}, u32[]{:S(2)}) collective-permute-start(bf16[8,2,128,1024]{3,2,1,0:T(8,128)(2,1)} %fusion.14), channel_id=1, source_target_pairs={{0,1},{1,0},{2,3},{3,2},{4,5},{5,4},{6,7},{7,6},{8,9},{9,8},{10,11... | collective-permute-start | bytes 12582920 | tf_op jit(solution)/shard_map/ppermute | solution.py:23
  1011.5 23.3 %collective-permute-start.51 = (bf16[128,1024]{0,1:T(8,128)(2,1)}, bf16[128,1024]{0,1:T(8,128)(2,1)}, u32[]{:S(2)}, u32[]{:S(2)}) collective-permute-start(bf16[128,1024]{0,1:T(8,128)(2,1)} %get-tuple-element.80), channel_id=1, source_target_pairs={{0,24},{4,28},{8,16},{12,20},{16,8},{20,12},{24,0},{28,4},{1,25},{... | collective-permute-start | bytes 786440 | tf_op jit(solution)/shard_map/ppermute | solution.py:36
  1015.9 22.1 %collective-permute-start.56 = (bf16[128,1024]{1,0:T(8,128)(2,1)}, bf16[128,1024]{1,0:T(8,128)(2,1)}, u32[]{:S(2)}, u32[]{:S(2)}) collective-permute-start(bf16[128,1024]{1,0:T(8,128)(2,1)} %get-tuple-element.75), channel_id=1, source_target_pairs={{0,8},{4,12},{8,0},{12,4},{16,24},{20,28},{24,16},{28,20},{1,9},{5... | collective-permute-start | bytes 786440 | tf_op jit(solution)/shard_map/ppermute | solution.py:36
  1018.1 44.3 %all-to-all-start.4 = ((f32[32,1,1141]{2,1,0:T(1,128)}), f32[32,1,1141]{2,1,0:T(1,128)S(1)}, u32[]{:S(2)}, u32[]{:S(2)}) async-start(f32[32,1,1141]{2,1,0:T(1,128)} %all_to_all.32), calls=%async_computation.4 | async-start | bytes 294912 | tf_op jit(solution)/shard_map/all_to_all | solution.py:40
  1025.6 28.2 %collective-permute-start.57 = (bf16[128,1024]{1,0:T(8,128)(2,1)}, bf16[128,1024]{1,0:T(8,128)(2,1)S(1)}, u32[]{:S(2)}, u32[]{:S(2)}) collective-permute-start(bf16[128,1024]{1,0:T(8,128)(2,1)} %get-tuple-element.76), channel_id=1, source_target_pairs={{0,16},{4,20},{8,24},{12,28},{16,0},{20,4},{24,8},{28,12},{1,17},{... | collective-permute-start | bytes 786440 | tf_op jit(solution)/shard_map/ppermute | solution.py:36
  1027.8 32.6 %collective-permute-start.58 = (bf16[128,1024]{1,0:T(8,128)(2,1)}, bf16[128,1024]{1,0:T(8,128)(2,1)S(1)}, u32[]{:S(2)}, u32[]{:S(2)}) collective-permute-start(bf16[128,1024]{1,0:T(8,128)(2,1)} %get-tuple-element.77), channel_id=1, source_target_pairs={{0,24},{4,28},{8,16},{12,20},{16,8},{20,12},{24,0},{28,4},{1,25},{... | collective-permute-start | bytes 786440 | tf_op jit(solution)/shard_map/ppermute | solution.py:36
  1034.8 29.8 %collective-permute-start.29 = (bf16[2,3,64,1024]{3,2,1,0:T(8,128)(2,1)}, bf16[2,3,64,1024]{3,2,1,0:T(8,128)(2,1)}, u32[]{:S(2)}, u32[]{:S(2)}) collective-permute-start(bf16[2,3,64,1024]{3,2,1,0:T(8,128)(2,1)} %pad_maximum_fusion.21), channel_id=1, source_target_pairs={{0,2},{1,3},{2,0},{3,1},{4,6},{5,7},{6,4},{7,5},{8,10},{9,11},{10,... | collective-permute-start | bytes 2359304 | tf_op jit(solution)/shard_map/ppermute | solution.py:23
  1038.0 29.6 %collective-permute-start.35 = (bf16[2,3,64,1024]{3,2,1,0:T(8,128)(2,1)}, bf16[2,3,64,1024]{3,2,1,0:T(8,128)(2,1)S(1)}, u32[]{:S(2)}, u32[]{:S(2)}) collective-permute-start(bf16[2,3,64,1024]{3,2,1,0:T(8,128)(2,1)} %pad_maximum_fusion.23), channel_id=1, source_target_pairs={{0,2},{1,3},{2,0},{3,1},{4,6},{5,7},{6,4},{7,5},{8,10},{9,11},{10,... | collective-permute-start | bytes 2359304 | tf_op jit(solution)/shard_map/ppermute | solution.py:23
  1077.3 22.9 %collective-permute-start.38 = (bf16[4,2,128,512]{3,2,0,1:T(8,128)(2,1)S(1)}, bf16[4,2,128,512]{3,2,0,1:T(8,128)(2,1)S(1)}, u32[]{:S(2)}, u32[]{:S(2)}) collective-permute-start(bf16[4,2,128,512]{3,2,0,1:T(8,128)(2,1)S(1)} %copy_bitcast_fusion.2), channel_id=1, source_target_pairs={{0,4},{4,0},{8,12},{12,8},{16,20},{20,16},{24,28},{28,24},{1,5},{5... | collective-permute-start | bytes 3145736 | tf_op jit(solution)/shard_map/ppermute | solution.py:36
  1078.5 22.8 %collective-permute-start.40 = (bf16[4,2,128,512]{3,2,0,1:T(8,128)(2,1)S(1)}, bf16[4,2,128,512]{3,2,0,1:T(8,128)(2,1)S(1)}, u32[]{:S(2)}, u32[]{:S(2)}) collective-permute-start(bf16[4,2,128,512]{3,2,0,1:T(8,128)(2,1)S(1)} %copy_bitcast_fusion.3), channel_id=1, source_target_pairs={{0,2},{1,3},{2,0},{3,1},{4,6},{5,7},{6,4},{7,5},{8,10},{9,11},{10,... | collective-permute-start | bytes 3145736 | tf_op jit(solution)/shard_map/ppermute | solution.py:23
  1115.9 21.1 %collective-permute-start.44 = (bf16[128,1024]{1,0:T(8,128)(2,1)S(1)}, bf16[128,1024]{1,0:T(8,128)(2,1)S(1)}, u32[]{:S(2)}, u32[]{:S(2)}) collective-permute-start(bf16[128,1024]{1,0:T(8,128)(2,1)S(1)} %get-tuple-element.83), channel_id=1, source_target_pairs={{0,24},{4,28},{8,16},{12,20},{16,8},{20,12},{24,0},{28,4},{1,25},{... | collective-permute-start | bytes 786440 | tf_op jit(solution)/shard_map/ppermute | solution.py:36
  (125 other events, 3032.6 us)
